TPU v7x, 512 devices: a whole 4x4x16 slice. The times are simulated.
512 devices in a mesh: section: 8 (over z_lo, core), seq: 64 (over y, z_hi, x).
Axes of the slice: x: 4, y: 4, z: 16 (z_hi: 4, z_lo: 4; z = z_hi * 4 + z_lo), core: 2. Of those that a mesh axis runs over, the one named last changes fastest.
Arguments:
- x_saved: bfloat16 [8, 2, 8192, 1024], P('section', None, 'seq'), may hold values from -6 to 6
- queries: bfloat16 [8, 2, 8192, 1024], P('section', None, 'seq'), may hold values from -30 to 30
- keys: bfloat16 [8, 2, 8192, 1024], P('section', None, 'seq'), may hold values from -30 to 30
- value_weight: bfloat16 [8, 1024, 1024], P('section', 'seq'), may hold values from -0.1875 to 0.1875
- out_weight: bfloat16 [8, 1024, 1024], P('section', 'seq'), may hold values from -0.1875 to 0.1875
- out_grad: bfloat16 [2, 8192, 1024], P(None, 'seq'), may hold values from -6 to 6
Outputs:
- section_grads: bfloat16 [8, 2, 8192, 1024], P('section', None, 'seq')
- query_grads: bfloat16 [8, 2, 8192, 1024], P('section', None, 'seq')
- key_grads: bfloat16 [8, 2, 8192, 1024], P('section', None, 'seq')
All inputs are finite; a program needn't handle non-finite values.
Results may differ from a plain program's by a relative error of at most 0.025.
Values may be sent and summed in bfloat16 or wider, within the bound.
A program may use at most 128 MiB of HBM per device.

v0:
```python
import math

import jax
import jax.numpy as jnp
from jax import lax
from jax.sharding import PartitionSpec as P

HEADS = 8


def from_partner(value, axis, stride):
    mask = 2**stride
    pairs = [(source, source ^ mask) for source in range(lax.axis_size(axis))]
    return lax.ppermute(value, axis, pairs)


def from_behind(block, axis, distance):
    devices = range(lax.axis_size(axis))
    route = [(i - distance, i) for i in devices if i - distance in devices]
    return lax.ppermute(block, axis, route)


def pick(array, index):
    return lax.dynamic_index_in_dim(array, index, 0, keepdims=False)


def place(array, piece, index, active):
    updated = lax.dynamic_update_index_in_dim(array, piece, index, 0)
    return jnp.where(active, updated, array)


def mirror(piece, n_section):
    bit_count = n_section.bit_length() - 1
    for bit_index in range(bit_count):
        piece = from_partner(piece, "section", bit_index)
    return piece


def per_device(x_saved, queries, keys, value_weight, out_weight, out_grad):
    n_section = lax.axis_size("section")
    section_pos = lax.axis_index("section")
    seq_first = lax.axis_index("seq") == 0
    upper_half = section_pos >= n_section // 2
    value_full, out_full = (
        lax.all_gather(value_weight, "seq", axis=1, tiled=True),
        lax.all_gather(out_weight, "seq", axis=1, tiled=True),
    )
    value_full = value_full[0]
    out_full = out_full[0]
    x_own = x_saved[0]
    x_mirror = mirror(x_own, n_section)
    x_here = jnp.where(
        upper_half,
        (x_own.astype(jnp.float32) + x_mirror.astype(jnp.float32)).astype(jnp.bfloat16),
        x_own,
    )
    query_here = queries[0]
    key_here = keys[0]
    micro_count, row_count, model_width = x_here.shape
    inner_width = query_here.shape[-1]
    head_size = inner_width // HEADS
    score_scale = 1.0 / math.sqrt(head_size)
    values = jnp.einsum(
        "mrd,di->mri", x_here, value_full, preferred_element_type=jnp.float32
    ).astype(jnp.bfloat16)
    key_prior, value_prior = from_behind((key_here, values), "seq", 1)
    row_index = jnp.arange(row_count)[:, None]
    col_index = jnp.arange(2 * row_count)[None, :]
    own_mask = (col_index >= row_count) & (col_index - row_count <= row_index)
    prior_mask = (col_index < row_count) & (col_index > row_index)
    allowed = (own_mask | prior_mask & jnp.logical_not(seq_first))[None]
    contract_last = (((1,), (1,)), ((), ()))

    def attend(incoming, micro_index):
        query_rows = pick(query_here, micro_index).reshape(row_count, HEADS, head_size)
        key_pairs = jnp.concatenate([pick(key_prior, micro_index), pick(key_here, micro_index)], 0)
        key_pairs = key_pairs.reshape(2 * row_count, HEADS, head_size)
        value_pairs = jnp.concatenate(
            [pick(value_prior, micro_index), pick(values, micro_index)], 0
        )
        value_pairs = value_pairs.reshape(2 * row_count, HEADS, head_size)
        value_grad_in = lax.dot_general(
            incoming, out_full, contract_last, preferred_element_type=jnp.float32
        )
        grad_rows = value_grad_in.astype(jnp.bfloat16).reshape(row_count, HEADS, head_size)
        scores = (
            jnp.einsum("rhd,chd->hrc", query_rows, key_pairs, preferred_element_type=jnp.float32)
            * score_scale
        )
        scores = jnp.where(allowed, scores, -1e30)
        row_max = jnp.max(scores, axis=-1, keepdims=True)
        exponent = jnp.where(allowed, jnp.exp(scores - row_max), 0.0)
        probabilities = exponent / jnp.sum(exponent, axis=-1, keepdims=True)
        prob_rounded = probabilities.astype(jnp.bfloat16)
        attended = jnp.einsum(
            "hrc,chd->rhd", prob_rounded, value_pairs, preferred_element_type=jnp.float32
        )
        row_delta = jnp.sum(grad_rows.astype(jnp.float32) * attended, axis=-1)
        dprob = jnp.einsum(
            "rhd,chd->hrc", grad_rows, value_pairs, preferred_element_type=jnp.float32
        )
        score_grad = (probabilities * (dprob - row_delta.T[:, :, None]) * score_scale).astype(
            jnp.bfloat16
        )
        query_grad = jnp.einsum(
            "hrc,chd->rhd", score_grad, key_pairs, preferred_element_type=jnp.float32
        )
        query_grad = query_grad.reshape(row_count, inner_width).astype(jnp.bfloat16)
        key_pairs_grad = jnp.einsum(
            "hrc,rhd->chd", score_grad, query_rows, preferred_element_type=jnp.float32
        )
        key_pairs_grad = key_pairs_grad.reshape(2 * row_count, inner_width)
        value_pairs_grad = jnp.einsum(
            "hrc,rhd->chd", prob_rounded, grad_rows, preferred_element_type=jnp.float32
        )
        value_pairs_grad = value_pairs_grad.reshape(2 * row_count, inner_width)
        return (
            value_pairs_grad[:row_count],
            value_pairs_grad[row_count:],
            query_grad,
            key_pairs_grad[row_count:],
            key_pairs_grad[:row_count],
        )

    def spare_attend(incoming, micro_index):
        zero_grad = jnp.zeros((row_count, inner_width), jnp.float32)
        return (
            zero_grad,
            zero_grad,
            jnp.zeros((row_count, inner_width), jnp.bfloat16),
            zero_grad,
            zero_grad,
        )

    def combine(incoming, value_grad, skipped):
        input_part = lax.dot_general(
            value_grad.astype(jnp.bfloat16),
            value_full,
            contract_last,
            preferred_element_type=jnp.float32,
        )
        return (incoming.astype(jnp.float32) + input_part + skipped.astype(jnp.float32)).astype(
            jnp.bfloat16
        )

    def spare_combine(incoming, value_grad, skipped):
        return jnp.zeros_like(incoming)

    tick_count = n_section + micro_count - 1
    received = jnp.zeros((row_count, model_width), jnp.bfloat16)
    skip_store = jnp.zeros((micro_count, row_count, model_width), jnp.bfloat16)
    grad_store = jnp.zeros((micro_count, row_count, model_width), jnp.bfloat16)
    query_store = jnp.zeros((micro_count, row_count, inner_width), jnp.bfloat16)
    key_store = jnp.zeros((micro_count, row_count, inner_width), jnp.float32)
    key_outgoing = jnp.zeros((micro_count, row_count, inner_width), jnp.bfloat16)
    for tick_index in range(tick_count):
        micro_index = tick_index - (n_section - 1) + section_pos
        active = (micro_index >= 0) & (micro_index < micro_count)
        micro_clip = jnp.clip(micro_index, 0, micro_count - 1)
        top_grad = pick(out_grad, micro_clip)
        incoming = jnp.where(section_pos == n_section - 1, top_grad, received)
        value_prior_grad, value_own_grad, query_grad, key_own_grad, key_prior_grad = lax.cond(
            active, attend, spare_attend, incoming, micro_clip
        )
        value_next_grad = from_behind(value_prior_grad.astype(jnp.bfloat16), "seq", -1)
        key_store = place(key_store, key_own_grad, micro_clip, active)
        key_outgoing = place(key_outgoing, key_prior_grad.astype(jnp.bfloat16), micro_clip, active)
        skipped = jnp.where(upper_half, jnp.zeros_like(top_grad), pick(skip_store, micro_clip))
        section_grad = lax.cond(
            active,
            combine,
            spare_combine,
            incoming,
            value_own_grad + value_next_grad.astype(jnp.float32),
            skipped,
        )
        grad_store = place(grad_store, section_grad, micro_clip, active)
        query_store = place(query_store, query_grad, micro_clip, active)
        if tick_index <= n_section // 2:
            arrived = mirror(section_grad, n_section)
            target = tick_index - section_pos
            accept = jnp.logical_not(upper_half) & (target >= 0) & (target < micro_count)
            skip_store = place(skip_store, arrived, jnp.clip(target, 0, micro_count - 1), accept)
        if tick_index < tick_count - 1:
            received = from_behind(section_grad, "section", -1)
    key_final = key_store + from_behind(key_outgoing, "seq", -1).astype(jnp.float32)
    return (grad_store[None], query_store[None], key_final.astype(jnp.bfloat16)[None])


def solution(mesh):
    placed = (
        P("section", None, "seq", None),
        P("section", None, "seq", None),
        P("section", None, "seq", None),
        P("section", "seq", None),
        P("section", "seq", None),
        P(None, "seq", None),
    )
    return jax.shard_map(
        per_device,
        mesh=mesh,
        in_specs=placed,
        out_specs=(
            P("section", None, "seq", None),
            P("section", None, "seq", None),
            P("section", None, "seq", None),
        ),
        check_vma=False,
    )
```

profile of v0, /device:TPU:6, one launch (start us, length us, event | category | flops | bytes accessed | tf_op | source)
XLA Modules:
  0.0 998.9 jit_solution(14796440225657033256)
XLA Ops:
  8.7 1.9 collective-permute-start.1
  10.6 2.1 collective-permute-done.1
  12.7 3.8 collective-permute-start.2
  16.5 12.2 %collective-permute-done.2 = bf16[2,128,1024]{2,1,0:T(8,128)(2,1)S(1)} collective-permute-done((bf16[2,128,1024]{2,1,0:T(8,128)(2,1)S(1)}, bf16[2,128,1024]{2,1,0:T(8,128)(2,1)S(1)}, u32[]{:S(2)}, u32[]{:S(2)}) %collective-permute-start.2) | collective-permute-done | bytes 524320 | tf_op jit(solution)/shard_map/ppermute | solution.py:14
  28.7 5.2 collective-permute-start.3
  35.2 9.0 collective-permute-start
  44.2 2.0 copy.198
  46.3 23.5 %collective-permute-done.3 = bf16[2,128,1024]{2,1,0:T(8,128)(2,1)S(1)} collective-permute-done((bf16[2,128,1024]{2,1,0:T(8,128)(2,1)S(1)}, bf16[2,128,1024]{2,1,0:T(8,128)(2,1)S(1)}, u32[]{:S(2)}, u32[]{:S(2)}) %collective-permute-start.3) | collective-permute-done | bytes 524320 | tf_op jit(solution)/shard_map/ppermute | solution.py:14
  70.6 106.7 %all-gather.5.cloned.1.call-done = bf16[1,1024,1024]{2,1,0:T(8,128)(2,1)} async-done(((bf16[1,16,1024]{2,1,0:T(8,128)(2,1)}), bf16[1,1024,1024]{2,1,0:T(8,128)(2,1)}) %all-gather.5.cloned.1.call-update) | async-done | bytes 2097168 | tf_op jit(solution)/shard_map/all_gather | solution.py:45
  177.3 2.5 fusion.219
  179.8 2.2 collective-permute-start.4
  182.9 131.3 %all-gather.3.cloned.1.call-done = bf16[1,1024,1024]{2,1,0:T(8,128)(2,1)} async-done(((bf16[1,16,1024]{2,1,0:T(8,128)(2,1)}), bf16[1,1024,1024]{2,1,0:T(8,128)(2,1)}) %all-gather.3.cloned.1.call-update) | async-done | bytes 2097168 | tf_op jit(solution)/shard_map/all_gather | solution.py:46
  314.2 3.3 conditional.18
  317.5 2.0 copy.202
  319.5 2.8 collective-permute-start.5
  322.2 25.1 %collective-permute-done.5 = bf16[128,1024]{1,0:T(8,128)(2,1)S(1)} collective-permute-done((bf16[128,1024]{1,0:T(8,128)(2,1)}, bf16[128,1024]{1,0:T(8,128)(2,1)S(1)}, u32[]{:S(2)}, u32[]{:S(2)}) %collective-permute-start.5) | collective-permute-done | bytes 262176 | tf_op jit(solution)/shard_map/ppermute | solution.py:20
  353.5 4.1 collective-permute-start.9
  359.6 4.2 conditional.20
  367.6 23.9 %collective-permute-start.10 = (bf16[128,1024]{1,0:T(8,128)(2,1)}, bf16[128,1024]{1,0:T(8,128)(2,1)S(1)}, u32[]{:S(2)}, u32[]{:S(2)}) collective-permute-start(bf16[128,1024]{1,0:T(8,128)(2,1)} %collective-permute-done.9), channel_id=1, source_target_pairs={{0,256},{64,320},{128,384},{192,448},{256,0},{320,64},{384,128},{4... | collective-permute-start | bytes 786440 | tf_op jit(solution)/shard_map/ppermute | solution.py:14
  393.7 3.2 collective-permute-done.10
  399.3 3.9 collective-permute-start.13
  404.8 36.4 %collective-permute-start.14 = (bf16[128,1024]{1,0:T(8,128)(2,1)}, bf16[128,1024]{1,0:T(8,128)(2,1)}, u32[]{:S(2)}, u32[]{:S(2)}) collective-permute-start(bf16[128,1024]{1,0:T(8,128)(2,1)} %collective-permute-done.13), channel_id=1, source_target_pairs={{0,128},{64,192},{128,0},{192,64},{256,384},{320,448},{384,256},{4... | collective-permute-start | bytes 786440 | tf_op jit(solution)/shard_map/ppermute | solution.py:14
  442.2 4.4 conditional.22
  450.4 17.7 %collective-permute-start.15 = (bf16[128,1024]{1,0:T(8,128)(2,1)}, bf16[128,1024]{1,0:T(8,128)(2,1)S(1)}, u32[]{:S(2)}, u32[]{:S(2)}) collective-permute-start(bf16[128,1024]{1,0:T(8,128)(2,1)} %collective-permute-done.14), channel_id=1, source_target_pairs={{0,256},{64,320},{128,384},{192,448},{256,0},{320,64},{384,128},{4... | collective-permute-start | bytes 786440 | tf_op jit(solution)/shard_map/ppermute | solution.py:14
  472.7 2.9 collective-permute-done.15
  478.7 36.4 %collective-permute-start.18 = (bf16[128,1024]{1,0:T(8,128)(2,1)}, bf16[128,1024]{1,0:T(8,128)(2,1)}, u32[]{:S(2)}, u32[]{:S(2)}) collective-permute-start(bf16[128,1024]{1,0:T(8,128)(2,1)} %get-tuple-element.749), channel_id=1, source_target_pairs={{0,64},{64,0},{128,192},{192,128},{256,320},{320,256},{384,448},{4... | collective-permute-start | bytes 786440 | tf_op jit(solution)/shard_map/ppermute | solution.py:14
  520.1 4.2 collective-permute-start.19
  525.2 4.0 conditional.24
  533.1 52.8 %collective-permute-start.20 = (bf16[128,1024]{1,0:T(8,128)(2,1)}, bf16[128,1024]{1,0:T(8,128)(2,1)S(1)}, u32[]{:S(2)}, u32[]{:S(2)}) collective-permute-start(bf16[128,1024]{1,0:T(8,128)(2,1)} %collective-permute-done.19), channel_id=1, source_target_pairs={{0,256},{64,320},{128,384},{192,448},{256,0},{320,64},{384,128},{4... | collective-permute-start | bytes 786440 | tf_op jit(solution)/shard_map/ppermute | solution.py:14
  590.2 2.4 collective-permute-done.20
  595.9 2.0 collective-permute-start.23
  602.8 4.6 collective-permute-start.24
  608.5 4.1 conditional.26
  616.5 53.1 %collective-permute-start.25 = (bf16[128,1024]{1,0:T(8,128)(2,1)}, bf16[128,1024]{1,0:T(8,128)(2,1)S(1)}, u32[]{:S(2)}, u32[]{:S(2)}) collective-permute-start(bf16[128,1024]{1,0:T(8,128)(2,1)} %collective-permute-done.24), channel_id=1, source_target_pairs={{0,256},{64,320},{128,384},{192,448},{256,0},{320,64},{384,128},{4... | collective-permute-start | bytes 786440 | tf_op jit(solution)/shard_map/ppermute | solution.py:14
  674.1 2.7 collective-permute-done.25
  679.9 2.0 collective-permute-start.28
  686.7 16.3 %collective-permute-start.29 = (bf16[128,1024]{1,0:T(8,128)(2,1)}, bf16[128,1024]{1,0:T(8,128)(2,1)}, u32[]{:S(2)}, u32[]{:S(2)}) collective-permute-start(bf16[128,1024]{1,0:T(8,128)(2,1)} %collective-permute-done.28), channel_id=1, source_target_pairs={{0,128},{64,192},{128,0},{192,64},{256,384},{320,448},{384,256},{4... | collective-permute-start | bytes 786440 | tf_op jit(solution)/shard_map/ppermute | solution.py:14
  705.6 4.0 conditional.28
  713.4 3.4 collective-permute-start.30
  720.5 14.9 %collective-permute-done.27 = bf16[128,1024]{1,0:T(8,128)(2,1)S(1)} collective-permute-done((bf16[128,1024]{1,0:T(8,128)(2,1)}, bf16[128,1024]{1,0:T(8,128)(2,1)S(1)}, u32[]{:S(2)}, u32[]{:S(2)}) %collective-permute-start.27) | collective-permute-done | bytes 262176 | tf_op jit(solution)/shard_map/ppermute | solution.py:20
  745.9 4.0 conditional.30
  757.4 9.0 collective-permute-done.32
  773.5 79.8 %collective-permute-done.33 = bf16[128,1024]{1,0:T(8,128)(2,1)S(1)} collective-permute-done((bf16[128,1024]{1,0:T(8,128)(2,1)}, bf16[128,1024]{1,0:T(8,128)(2,1)S(1)}, u32[]{:S(2)}, u32[]{:S(2)}) %collective-permute-start.33) | collective-permute-done | bytes 262176 | tf_op jit(solution)/shard_map/ppermute | solution.py:20
  855.0 37.6 %conditional.32 = (f32[128,1024]{0,1:T(8,128)}, f32[128,1024]{0,1:T(8,128)}, bf16[1,128,1024]{2,1,0:T(8,128)(2,1)}, f32[1,128,1024]{2,1,0:T(8,128)}, bf16[1,128,1024]{2,1,0:T(8,128)(2,1)}) conditional(s32[]{:T(128)} %convert_element_type.615, () %tuple.267, (bf16[128,1024]{1,0:T(8,128)(2,1)}, bf16[1024,1024]{1,0:T(8,128)(2,1)}, ...), branch_computations={%region_49.50_spmd, %region_50.54_spmd} | conditional | flops 679607552 | bytes 42000724 | solution.py:162
  857.9 3.2 convolution_convert_fusion.14
  874.9 2.7 fusion.250
  877.6 2.1 fusion.177
  884.5 2.3 fusion.249
  888.7 2.1 copy.335
  898.2 2.1 select_dynamic-update-slice_fusion.1
  900.3 12.7 %collective-permute-done.34 = bf16[128,1024]{1,0:T(8,128)(2,1)S(1)} collective-permute-done((bf16[128,1024]{1,0:T(8,128)(2,1)}, bf16[128,1024]{1,0:T(8,128)(2,1)S(1)}, u32[]{:S(2)}, u32[]{:S(2)}) %collective-permute-start.34) | collective-permute-done | bytes 262176 | tf_op jit(solution)/shard_map/ppermute | solution.py:20
  913.8 6.7 conditional.33
  913.8 2.1 copy.231
  915.9 2.9 fusion.191
  930.0 35.6 %conditional.34 = (f32[128,1024]{0,1:T(8,128)}, f32[128,1024]{0,1:T(8,128)}, bf16[1,128,1024]{2,1,0:T(8,128)(2,1)}, f32[1,128,1024]{2,1,0:T(8,128)}, bf16[1,128,1024]{2,1,0:T(8,128)(2,1)}) conditional(s32[]{:T(128)} %convert_element_type.618, () %tuple.271, (bf16[128,1024]{1,0:T(8,128)(2,1)}, bf16[1024,1024]{1,0:T(8,128)(2,1)}, ...), branch_computations={%region_56.57_spmd, %region_57.61_spmd} | conditional | flops 679607552 | bytes 46195108 | solution.py:162
  932.7 3.3 convolution_convert_fusion.16
  948.2 2.6 fusion.252
  961.7 2.0 copy.341
  965.6 2.0 copy.234
  976.2 5.9 collective-permute-done.36
  982.9 4.9 conditional.35
  982.9 2.0 copy.235
  984.9 2.9 fusion.216
  989.6 2.0 fusion.224
  (309 shorter events, 228.9 us)
Async XLA Ops:
  7.2 170.1 %copy-start.96 = (bf16[1,2,128,1024]{3,2,1,0:T(8,128)(2,1)S(1)}, bf16[1,2,128,1024]{3,2,1,0:T(8,128)(2,1)}, u32[]{:S(2)}) copy-start(bf16[1,2,128,1024]{3,2,1,0:T(8,128)(2,1)} %param.42) | copy-start | bytes 1572868
  7.2 170.1 %all-gather.5.cloned.1.call-start = ((), (), s32[]{:S(2)}) async-start(), calls=%async_computation.1 | async-start | bytes 2129920 | tf_op jit(solution)/shard_map/all_gather | solution.py:45
  7.9 306.3 %all-gather.3.cloned.1.call-start = ((), (), s32[]{:S(2)}) async-start(), calls=%async_computation | async-start | bytes 2129920 | tf_op jit(solution)/shard_map/all_gather | solution.py:46
  8.7 4.0 collective-permute-start.1
  12.7 16.0 %collective-permute-start.2 = (bf16[2,128,1024]{2,1,0:T(8,128)(2,1)S(1)}, bf16[2,128,1024]{2,1,0:T(8,128)(2,1)S(1)}, u32[]{:S(2)}, u32[]{:S(2)}) collective-permute-start(bf16[2,128,1024]{2,1,0:T(8,128)(2,1)S(1)} %collective-permute-done.1), channel_id=1, source_target_pairs={{0,128},{64,192},{128,0},{192,64},{256,384},{320,448},{384,256},{4... | collective-permute-start | bytes 1572872 | tf_op jit(solution)/shard_map/ppermute | solution.py:14
  28.7 41.1 %collective-permute-start.3 = (bf16[2,128,1024]{2,1,0:T(8,128)(2,1)S(1)}, bf16[2,128,1024]{2,1,0:T(8,128)(2,1)S(1)}, u32[]{:S(2)}, u32[]{:S(2)}) collective-permute-start(bf16[2,128,1024]{2,1,0:T(8,128)(2,1)S(1)} %collective-permute-done.2), channel_id=1, source_target_pairs={{0,256},{64,320},{128,384},{192,448},{256,0},{320,64},{384,128},{4... | collective-permute-start | bytes 1572872 | tf_op jit(solution)/shard_map/ppermute | solution.py:14
  35.2 144.6 %copy-start.7 = (bf16[1,2,128,1024]{2,3,1,0:T(8,128)(2,1)}, bf16[1,2,128,1024]{2,3,1,0:T(8,128)(2,1)S(1)}, u32[]{:S(2)}) copy-start(bf16[1,2,128,1024]{2,3,1,0:T(8,128)(2,1)S(1)} %copy.199) | copy-start | bytes 1572868
  35.2 147.6 %collective-permute-start = (bf16[2,128,1024]{1,2,0:T(8,128)(2,1)S(1)}, bf16[2,128,1024]{1,2,0:T(8,128)(2,1)S(1)}, u32[]{:S(2)}, u32[]{:S(2)}) collective-permute-start(bf16[2,128,1024]{1,2,0:T(8,128)(2,1)S(1)} %bitcast.435), channel_id=1, source_target_pairs={{0,1},{1,2},{2,3},{3,4},{4,5},{5,6},{6,7},{7,8},{8,9},{9,10},{10,1... | collective-permute-start | bytes 1572872 | tf_op jit(solution)/shard_map/ppermute | solution.py:20
  46.3 135.7 %copy-start.14 = (bf16[2,128,1024]{2,1,0:T(8,128)(2,1)S(1)}, bf16[2,128,1024]{2,1,0:T(8,128)(2,1)}, u32[]{:S(2)}) copy-start(bf16[2,128,1024]{2,1,0:T(8,128)(2,1)} %param.47) | copy-start | bytes 1572868
  179.8 134.4 %collective-permute-start.4 = (bf16[2,128,1024]{2,1,0:T(8,128)(2,1)S(1)}, bf16[2,128,1024]{2,1,0:T(8,128)(2,1)S(1)}, u32[]{:S(2)}, u32[]{:S(2)}) collective-permute-start(bf16[2,128,1024]{2,1,0:T(8,128)(2,1)S(1)} %fusion.219), channel_id=1, source_target_pairs={{0,1},{1,2},{2,3},{3,4},{4,5},{5,6},{6,7},{7,8},{8,9},{9,10},{10,1... | collective-permute-start | bytes 1572872 | tf_op jit(solution)/shard_map/ppermute | solution.py:20
  182.8 131.3 %copy-start.20 = (bf16[2,128,1024]{1,2,0:T(8,128)(2,1)}, bf16[2,128,1024]{1,2,0:T(8,128)(2,1)S(1)}, u32[]{:S(2)}) copy-start(bf16[2,128,1024]{1,2,0:T(8,128)(2,1)S(1)} %collective-permute-done) | copy-start | bytes 1572868
  314.2 34.0 %copy-start = (bf16[1,1024,1024]{2,1,0:T(8,128)(2,1)S(1)}, bf16[1,1024,1024]{2,1,0:T(8,128)(2,1)}, u32[]{:S(2)}) copy-start(bf16[1,1024,1024]{2,1,0:T(8,128)(2,1)} %all-gather.5.cloned.1.call-done) | copy-start | bytes 6291460
  317.5 30.7 %copy-start.29 = (bf16[1,128,1024]{2,1,0:T(8,128)(2,1)}, bf16[1,128,1024]{2,1,0:T(8,128)(2,1)S(1)}, u32[]{:S(2)}) copy-start(bf16[1,128,1024]{2,1,0:T(8,128)(2,1)S(1)} %get-tuple-element.1020) | copy-start | bytes 786436
  319.5 27.9 %collective-permute-start.5 = (bf16[128,1024]{1,0:T(8,128)(2,1)}, bf16[128,1024]{1,0:T(8,128)(2,1)S(1)}, u32[]{:S(2)}, u32[]{:S(2)}) collective-permute-start(bf16[128,1024]{1,0:T(8,128)(2,1)} %copy.202), channel_id=1, source_target_pairs={{1,0},{2,1},{3,2},{4,3},{5,4},{6,5},{7,6},{8,7},{9,8},{10,9},{11,1... | collective-permute-start | bytes 786440 | tf_op jit(solution)/shard_map/ppermute | solution.py:20
  349.7 3.8 collective-permute-start.8
  351.7 6.2 collective-permute-start.6
  353.5 14.1 %collective-permute-start.9 = (bf16[128,1024]{1,0:T(8,128)(2,1)}, bf16[128,1024]{1,0:T(8,128)(2,1)}, u32[]{:S(2)}, u32[]{:S(2)}) collective-permute-start(bf16[128,1024]{1,0:T(8,128)(2,1)} %collective-permute-done.8), channel_id=1, source_target_pairs={{0,128},{64,192},{128,0},{192,64},{256,384},{320,448},{384,256},{4... | collective-permute-start | bytes 786440 | tf_op jit(solution)/shard_map/ppermute | solution.py:14
  365.7 27.0 %collective-permute-start.7 = (bf16[128,1024]{1,0:T(8,128)(2,1)}, bf16[128,1024]{1,0:T(8,128)(2,1)S(1)}, u32[]{:S(2)}, u32[]{:S(2)}) collective-permute-start(bf16[128,1024]{1,0:T(8,128)(2,1)} %copy.206), channel_id=1, source_target_pairs={{1,0},{2,1},{3,2},{4,3},{5,4},{6,5},{7,6},{8,7},{9,8},{10,9},{11,1... | collective-permute-start | bytes 786440 | tf_op jit(solution)/shard_map/ppermute | solution.py:20
  367.6 29.3 %collective-permute-start.10 = (bf16[128,1024]{1,0:T(8,128)(2,1)}, bf16[128,1024]{1,0:T(8,128)(2,1)S(1)}, u32[]{:S(2)}, u32[]{:S(2)}) collective-permute-start(bf16[128,1024]{1,0:T(8,128)(2,1)} %collective-permute-done.9), channel_id=1, source_target_pairs={{0,256},{64,320},{128,384},{192,448},{256,0},{320,64},{384,128},{4... | collective-permute-start | bytes 786440 | tf_op jit(solution)/shard_map/ppermute | solution.py:14
  392.7 5.8 copy-start.1
  399.3 3.9 copy-start.30
  399.3 41.9 %copy-start.10 = (bf16[2,128,1024]{2,1,0:T(8,128)(2,1)S(1)}, bf16[2,128,1024]{2,1,0:T(8,128)(2,1)}, u32[]{:S(2)}) copy-start(bf16[2,128,1024]{2,1,0:T(8,128)(2,1)} %copy-done.9) | copy-start | bytes 1572868
  399.3 42.0 %copy-start.15 = (bf16[2,128,1024]{2,1,0:T(8,128)(2,1)S(1)}, bf16[2,128,1024]{2,1,0:T(8,128)(2,1)}, u32[]{:S(2)}) copy-start(bf16[2,128,1024]{2,1,0:T(8,128)(2,1)} %param.47) | copy-start | bytes 1572868
  399.3 5.5 collective-permute-start.13
  403.3 38.0 %collective-permute-start.11 = (bf16[128,1024]{1,0:T(8,128)(2,1)}, bf16[128,1024]{1,0:T(8,128)(2,1)S(1)}, u32[]{:S(2)}, u32[]{:S(2)}) collective-permute-start(bf16[128,1024]{1,0:T(8,128)(2,1)} %get-tuple-element.745), channel_id=1, source_target_pairs={{64,0},{128,64},{192,128},{256,192},{320,256},{384,320},{448,384},... | collective-permute-start | bytes 786440 | tf_op jit(solution)/shard_map/ppermute | solution.py:20
  404.8 37.4 %copy-start.3 = (bf16[2,128,1024]{2,1,0:T(8,128)(2,1)}, bf16[2,128,1024]{2,1,0:T(8,128)(2,1)S(1)}, u32[]{:S(2)}) copy-start(bf16[2,128,1024]{2,1,0:T(8,128)(2,1)S(1)} %select_dynamic-update-slice_fusion.33) | copy-start | bytes 1572868
  404.8 45.6 %collective-permute-start.14 = (bf16[128,1024]{1,0:T(8,128)(2,1)}, bf16[128,1024]{1,0:T(8,128)(2,1)}, u32[]{:S(2)}, u32[]{:S(2)}) collective-permute-start(bf16[128,1024]{1,0:T(8,128)(2,1)} %collective-permute-done.13), channel_id=1, source_target_pairs={{0,128},{64,192},{128,0},{192,64},{256,384},{320,448},{384,256},{4... | collective-permute-start | bytes 786440 | tf_op jit(solution)/shard_map/ppermute | solution.py:14
  448.5 23.3 %collective-permute-start.12 = (bf16[128,1024]{1,0:T(8,128)(2,1)}, bf16[128,1024]{1,0:T(8,128)(2,1)S(1)}, u32[]{:S(2)}, u32[]{:S(2)}) collective-permute-start(bf16[128,1024]{1,0:T(8,128)(2,1)} %copy.210), channel_id=1, source_target_pairs={{1,0},{2,1},{3,2},{4,3},{5,4},{6,5},{7,6},{8,7},{9,8},{10,9},{11,1... | collective-permute-start | bytes 786440 | tf_op jit(solution)/shard_map/ppermute | solution.py:20
  450.4 25.1 %collective-permute-start.15 = (bf16[128,1024]{1,0:T(8,128)(2,1)}, bf16[128,1024]{1,0:T(8,128)(2,1)S(1)}, u32[]{:S(2)}, u32[]{:S(2)}) collective-permute-start(bf16[128,1024]{1,0:T(8,128)(2,1)} %collective-permute-done.14), channel_id=1, source_target_pairs={{0,256},{64,320},{128,384},{192,448},{256,0},{320,64},{384,128},{4... | collective-permute-start | bytes 786440 | tf_op jit(solution)/shard_map/ppermute | solution.py:14
  478.7 45.5 %copy-start.12 = (bf16[2,128,1024]{2,1,0:T(8,128)(2,1)S(1)}, bf16[2,128,1024]{2,1,0:T(8,128)(2,1)}, u32[]{:S(2)}) copy-start(bf16[2,128,1024]{2,1,0:T(8,128)(2,1)} %copy-done.11) | copy-start | bytes 1572868
  478.7 45.6 %copy-start.16 = (bf16[2,128,1024]{2,1,0:T(8,128)(2,1)S(1)}, bf16[2,128,1024]{2,1,0:T(8,128)(2,1)}, u32[]{:S(2)}) copy-start(bf16[2,128,1024]{2,1,0:T(8,128)(2,1)} %param.47) | copy-start | bytes 1572868
  478.7 41.3 %collective-permute-start.18 = (bf16[128,1024]{1,0:T(8,128)(2,1)}, bf16[128,1024]{1,0:T(8,128)(2,1)}, u32[]{:S(2)}, u32[]{:S(2)}) collective-permute-start(bf16[128,1024]{1,0:T(8,128)(2,1)} %get-tuple-element.749), channel_id=1, source_target_pairs={{0,64},{64,0},{128,192},{192,128},{256,320},{320,256},{384,448},{4... | collective-permute-start | bytes 786440 | tf_op jit(solution)/shard_map/ppermute | solution.py:14
  516.9 7.5 collective-permute-start.16
  520.1 13.0 %collective-permute-start.19 = (bf16[128,1024]{1,0:T(8,128)(2,1)}, bf16[128,1024]{1,0:T(8,128)(2,1)}, u32[]{:S(2)}, u32[]{:S(2)}) collective-permute-start(bf16[128,1024]{1,0:T(8,128)(2,1)} %collective-permute-done.18), channel_id=1, source_target_pairs={{0,128},{64,192},{128,0},{192,64},{256,384},{320,448},{384,256},{4... | collective-permute-start | bytes 786440 | tf_op jit(solution)/shard_map/ppermute | solution.py:14
  531.1 58.3 %collective-permute-start.17 = (bf16[128,1024]{1,0:T(8,128)(2,1)}, bf16[128,1024]{1,0:T(8,128)(2,1)S(1)}, u32[]{:S(2)}, u32[]{:S(2)}) collective-permute-start(bf16[128,1024]{1,0:T(8,128)(2,1)} %copy.214), channel_id=1, source_target_pairs={{1,0},{2,1},{3,2},{4,3},{5,4},{6,5},{7,6},{8,7},{9,8},{10,9},{11,1... | collective-permute-start | bytes 786440 | tf_op jit(solution)/shard_map/ppermute | solution.py:20
  533.1 59.6 %collective-permute-start.20 = (bf16[128,1024]{1,0:T(8,128)(2,1)}, bf16[128,1024]{1,0:T(8,128)(2,1)S(1)}, u32[]{:S(2)}, u32[]{:S(2)}) collective-permute-start(bf16[128,1024]{1,0:T(8,128)(2,1)} %collective-permute-done.19), channel_id=1, source_target_pairs={{0,256},{64,320},{128,384},{192,448},{256,0},{320,64},{384,128},{4... | collective-permute-start | bytes 786440 | tf_op jit(solution)/shard_map/ppermute | solution.py:14
  595.9 11.6 %copy-start.5 = (bf16[2,128,1024]{2,1,0:T(8,128)(2,1)S(1)}, bf16[2,128,1024]{2,1,0:T(8,128)(2,1)}, u32[]{:S(2)}) copy-start(bf16[2,128,1024]{2,1,0:T(8,128)(2,1)} %select_dynamic-update-slice_fusion.23) | copy-start | bytes 1572868
  595.9 11.8 %copy-start.17 = (bf16[2,128,1024]{2,1,0:T(8,128)(2,1)S(1)}, bf16[2,128,1024]{2,1,0:T(8,128)(2,1)}, u32[]{:S(2)}) copy-start(bf16[2,128,1024]{2,1,0:T(8,128)(2,1)} %param.47) | copy-start | bytes 1572868
  595.9 7.0 collective-permute-start.23
  599.8 7.8 collective-permute-start.21
  602.8 13.6 %collective-permute-start.24 = (bf16[128,1024]{1,0:T(8,128)(2,1)}, bf16[128,1024]{1,0:T(8,128)(2,1)}, u32[]{:S(2)}, u32[]{:S(2)}) collective-permute-start(bf16[128,1024]{1,0:T(8,128)(2,1)} %collective-permute-done.23), channel_id=1, source_target_pairs={{0,128},{64,192},{128,0},{192,64},{256,384},{320,448},{384,256},{4... | collective-permute-start | bytes 786440 | tf_op jit(solution)/shard_map/ppermute | solution.py:14
  614.6 58.7 %collective-permute-start.22 = (bf16[128,1024]{1,0:T(8,128)(2,1)}, bf16[128,1024]{1,0:T(8,128)(2,1)S(1)}, u32[]{:S(2)}, u32[]{:S(2)}) collective-permute-start(bf16[128,1024]{1,0:T(8,128)(2,1)} %copy.218), channel_id=1, source_target_pairs={{1,0},{2,1},{3,2},{4,3},{5,4},{6,5},{7,6},{8,7},{9,8},{10,9},{11,1... | collective-permute-start | bytes 786440 | tf_op jit(solution)/shard_map/ppermute | solution.py:20
  616.5 60.2 %collective-permute-start.25 = (bf16[128,1024]{1,0:T(8,128)(2,1)}, bf16[128,1024]{1,0:T(8,128)(2,1)S(1)}, u32[]{:S(2)}, u32[]{:S(2)}) collective-permute-start(bf16[128,1024]{1,0:T(8,128)(2,1)} %collective-permute-done.24), channel_id=1, source_target_pairs={{0,256},{64,320},{128,384},{192,448},{256,0},{320,64},{384,128},{4... | collective-permute-start | bytes 786440 | tf_op jit(solution)/shard_map/ppermute | solution.py:14
  679.9 24.9 %copy-start.18 = (bf16[2,128,1024]{2,1,0:T(8,128)(2,1)S(1)}, bf16[2,128,1024]{2,1,0:T(8,128)(2,1)}, u32[]{:S(2)}) copy-start(bf16[2,128,1024]{2,1,0:T(8,128)(2,1)} %param.47) | copy-start | bytes 1572868
  679.9 6.8 collective-permute-start.28
  683.7 21.1 %collective-permute-start.26 = (bf16[128,1024]{1,0:T(8,128)(2,1)}, bf16[128,1024]{1,0:T(8,128)(2,1)S(1)}, u32[]{:S(2)}, u32[]{:S(2)}) collective-permute-start(bf16[128,1024]{1,0:T(8,128)(2,1)} %get-tuple-element.757), channel_id=1, source_target_pairs={{64,0},{128,64},{192,128},{256,192},{320,256},{384,320},{448,384},... | collective-permute-start | bytes 786440 | tf_op jit(solution)/shard_map/ppermute | solution.py:20
  686.7 26.6 %collective-permute-start.29 = (bf16[128,1024]{1,0:T(8,128)(2,1)}, bf16[128,1024]{1,0:T(8,128)(2,1)}, u32[]{:S(2)}, u32[]{:S(2)}) collective-permute-start(bf16[128,1024]{1,0:T(8,128)(2,1)} %collective-permute-done.28), channel_id=1, source_target_pairs={{0,128},{64,192},{128,0},{192,64},{256,384},{320,448},{384,256},{4... | collective-permute-start | bytes 786440 | tf_op jit(solution)/shard_map/ppermute | solution.py:14
  711.5 23.9 %collective-permute-start.27 = (bf16[128,1024]{1,0:T(8,128)(2,1)}, bf16[128,1024]{1,0:T(8,128)(2,1)S(1)}, u32[]{:S(2)}, u32[]{:S(2)}) collective-permute-start(bf16[128,1024]{1,0:T(8,128)(2,1)} %copy.222), channel_id=1, source_target_pairs={{1,0},{2,1},{3,2},{4,3},{5,4},{6,5},{7,6},{8,7},{9,8},{10,9},{11,1... | collective-permute-start | bytes 786440 | tf_op jit(solution)/shard_map/ppermute | solution.py:20
  713.4 22.8 %collective-permute-start.30 = (bf16[128,1024]{1,0:T(8,128)(2,1)}, bf16[128,1024]{1,0:T(8,128)(2,1)S(1)}, u32[]{:S(2)}, u32[]{:S(2)}) collective-permute-start(bf16[128,1024]{1,0:T(8,128)(2,1)} %collective-permute-done.29), channel_id=1, source_target_pairs={{0,256},{64,320},{128,384},{192,448},{256,0},{320,64},{384,128},{4... | collective-permute-start | bytes 786440 | tf_op jit(solution)/shard_map/ppermute | solution.py:14
  739.4 4.8 collective-permute-start.31
  751.8 14.6 %collective-permute-start.32 = (bf16[128,1024]{1,0:T(8,128)(2,1)}, bf16[128,1024]{1,0:T(8,128)(2,1)S(1)}, u32[]{:S(2)}, u32[]{:S(2)}) collective-permute-start(bf16[128,1024]{1,0:T(8,128)(2,1)} %copy.226), channel_id=1, source_target_pairs={{1,0},{2,1},{3,2},{4,3},{5,4},{6,5},{7,6},{8,7},{9,8},{10,9},{11,1... | collective-permute-start | bytes 786440 | tf_op jit(solution)/shard_map/ppermute | solution.py:20
  768.7 84.6 %collective-permute-start.33 = (bf16[128,1024]{1,0:T(8,128)(2,1)}, bf16[128,1024]{1,0:T(8,128)(2,1)S(1)}, u32[]{:S(2)}, u32[]{:S(2)}) collective-permute-start(bf16[128,1024]{1,0:T(8,128)(2,1)} %get-tuple-element.765), channel_id=1, source_target_pairs={{64,0},{128,64},{192,128},{256,192},{320,256},{384,320},{448,384},... | collective-permute-start | bytes 786440 | tf_op jit(solution)/shard_map/ppermute | solution.py:20
  880.2 2.5 copy-start.45
  894.5 18.5 %collective-permute-start.34 = (bf16[128,1024]{1,0:T(8,128)(2,1)}, bf16[128,1024]{1,0:T(8,128)(2,1)S(1)}, u32[]{:S(2)}, u32[]{:S(2)}) collective-permute-start(bf16[128,1024]{1,0:T(8,128)(2,1)} %copy.230), channel_id=1, source_target_pairs={{1,0},{2,1},{3,2},{4,3},{5,4},{6,5},{7,6},{8,7},{9,8},{10,9},{11,1... | collective-permute-start | bytes 786440 | tf_op jit(solution)/shard_map/ppermute | solution.py:20
  920.5 8.8 copy-start.19
  920.5 8.8 collective-permute-start.35
  932.7 7.9 copy-start.8
  938.8 9.4 copy-start.28
  943.6 7.2 copy-start.67
  945.5 5.3 copy-start.57
  948.2 2.6 copy-start.86
  965.6 9.4 copy-start.2
  967.6 14.5 %collective-permute-start.36 = (bf16[128,1024]{1,0:T(8,128)(2,1)}, bf16[128,1024]{1,0:T(8,128)(2,1)S(1)}, u32[]{:S(2)}, u32[]{:S(2)}) collective-permute-start(bf16[128,1024]{1,0:T(8,128)(2,1)} %copy.234), channel_id=1, source_target_pairs={{1,0},{2,1},{3,2},{4,3},{5,4},{6,5},{7,6},{8,7},{9,8},{10,9},{11,1... | collective-permute-start | bytes 786440 | tf_op jit(solution)/shard_map/ppermute | solution.py:20
  971.3 18.3 %collective-permute-start.37 = (bf16[2,128,1024]{2,1,0:T(8,128)(2,1)}, bf16[2,128,1024]{2,1,0:T(8,128)(2,1)}, u32[]{:S(2)}, u32[]{:S(2)}) collective-permute-start(bf16[2,128,1024]{2,1,0:T(8,128)(2,1)} %select_dynamic-update-slice_fusion.9), channel_id=1, source_target_pairs={{1,0},{2,1},{3,2},{4,3},{5,4},{6,5},{7,6},{8,7},{9,8},{10,9},{11,1... | collective-permute-start | bytes 1572872 | tf_op jit(solution)/shard_map/ppermute | solution.py:20
  (21 other events, 32.1 us)
Sparse Core Ops, SparseCore 0:
  12.2 165.0 all-gather.4
  181.5 132.6 all-gather.2
where the time goes:
time: 1010 us; the launch traced here: 999 us
  waiting for transfers between devices  436 us (43%)
  starting transfers between devices  315 us (31%)
  local copies, waits for them, and re-layouts  121 us (12%)
  other arithmetic  79.4 us (8%)
  matrix products  30.4 us (3%)
  between operations  15.5 us (2%)
    ppermute x18, starting transfers between devices, from_partner(): return lax.ppermute(value, axis, pairs)  274 us
    ppermute x20, waiting for transfers between devices, from_behind(): return lax.ppermute(block, axis, route)  147 us
    all_gather x1, waiting for transfers between devices, per_device(): lax.all_gather(out_weight, 'seq', axis=1, tiled=True)  131 us
    all_gather x1, waiting for transfers between devices, per_device(): lax.all_gather(value_weight, 'seq', axis=1, tiled=True)  107 us
    select_n x41, other arithmetic, place(): return jnp.where(active, updated, array)  59.8 us
    ppermute x18, waiting for transfers between devices, from_partner(): return lax.ppermute(value, axis, pairs)  49.5 us
    ppermute x20, starting transfers between devices, from_behind(): return lax.ppermute(block, axis, route)  41.6 us
    cond x15, local copies, waits for them, and re-layouts, per_device(): lax.cond(active, attend, spare_attend, incoming, micro_clip)  28.5 us
  transfers between devices with their start and end apart: 40, of which 16 were waited for; matrix products, arithmetic and copies ran while one was open for 11% of the time, Pallas kernels for 0%

commit v1 on v0

v1 whole, which is shorter than its diff:
```python
import functools
import math

import jax
import jax.numpy as jnp
from jax import lax
from jax.experimental import pallas as pl
from jax.experimental.pallas import tpu as pltpu
from jax.sharding import PartitionSpec as P

MESH = pl.DeviceIdType.MESH
HEADS = 8
HEAD = 128
ROWS = 128
SIDE = 4
CHUNKS = 4
BF16 = jnp.bfloat16
F32 = jnp.float32
NN = (((1,), (0,)), ((), ()))
NT = (((1,), (1,)), ((), ()))


def dot(left, right, dims=NN):
    return lax.dot_general(left, right, dims, preferred_element_type=F32)


def kernel(
    sections, blocks, width,
    x, q, k, wv, wo, og,
    sg, dq, dk,
    w, qv, kv, xv, ogv, qnext, kt, vals, xh, xmirror, weight, prob, grx, out, skip, acc, vgi, vg,
    stat, statrx, factor, bias, dprob, delta, deltarx, dqown, dqnext, dqrx, pass1, pass2,
    lsem, qsend, qrecv, e1send, e1recv, e2send, e2recv, e3send, e3recv, tsend, trecv, msend, mrecv, zsend, zrecv, rsend, rrecv, isend,
    gsend, grecv, ssend, srecv, esend, erecv, dsend, drecv, go_z, go_r,
):
    s = lax.axis_index("section")
    i = lax.axis_index("seq")
    cy = lax.div(i, SIDE * SIDE)
    cz = lax.rem(lax.div(i, SIDE), SIDE)
    cx = lax.rem(i, SIDE)
    after = lax.rem(i + 1, blocks)
    before = lax.rem(i + blocks - 1, blocks)
    top = sections - 1
    half = sections // 2
    mirror_s = top - s
    step = width // CHUNKS
    scale = 1.0 / math.sqrt(HEAD)

    def at(y, z, x_):
        return y * (SIDE * SIDE) + z * SIDE + x_

    def copy(src, dst, send, recv, device):
        return pltpu.make_async_remote_copy(
            src_ref=src, dst_ref=dst, send_sem=send, recv_sem=recv,
            device_id=device, device_id_type=MESH,
        )


    def local_copy(n):
        src, dst = (
            (q.at[0], qv), (k.at[0], kv), (wo.at[0], w.at[0, cy, cz, cx]),
            (wv.at[0], w.at[1, cy, cz, cx]), (x.at[0], xv), (og, ogv),
        )[n]
        return pltpu.make_async_copy(src, dst, lsem.at[n])

    def query_copy(m):
        return copy(q.at[0, m], qnext.at[m], qsend.at[m], qrecv.at[m], (s, before))


    quarter = ROWS // SIDE
    back = lax.rem(i + blocks - SIDE, blocks)

    def edge_out(j):
        src = q.at[0, :, pl.ds(j * quarter, quarter)]
        return copy(src, pass1, e1send.at[j], e1recv.at[0], (s, i + j))

    def edge_over(first, last):
        src = q.at[0, :, pl.ds(0, quarter)] if first else pass1
        if last:
            dst, sem = qnext.at[:, pl.ds((SIDE - 1) * quarter, quarter)], e3recv.at[SIDE - 1]
        else:
            dst, sem = pass2, e2recv.at[0]
        return copy(src, dst, e2send.at[0], sem, (s, back))

    def edge_in():
        rows = pl.ds(pl.multiple_of(cx * quarter, quarter), quarter)
        to = i - cx + SIDE - 1
        return copy(pass2, qnext.at[:, rows], e3send.at[0], e3recv.at[cx], (s, to))

    def edge_arrival(j):
        part = qnext.at[:, pl.ds(j * quarter, quarter)]
        return copy(part, part, e3send.at[0], e3recv.at[j], (s, i))

    def stat_copy(m, side):
        to = before if side == 0 else after
        return copy(
            stat.at[m, side], statrx.at[m, 1 - side], tsend.at[m, side], trecv.at[m, 1 - side], (s, to)
        )

    def delta_copy(m, side):
        to = before if side == 0 else after
        return copy(
            delta.at[m, side], deltarx.at[m, 1 - side], esend.at[m, side], erecv.at[m, 1 - side], (s, to)
        )

    def mirror_copy():
        return copy(x.at[0], xmirror, msend.at[0], mrecv.at[0], (mirror_s, i))

    def z_copy(a, d):
        to = at(cy, lax.rem(cz + d, SIDE), cx)
        src = (wo if a == 0 else wv).at[0]
        return copy(src, w.at[a, cy, cz, cx], zsend.at[a, d - 1], zrecv.at[a, d - 1], (s, to))

    def z_arrival(a, d):
        piece = w.at[a, cy, lax.rem(cz + SIDE - d, SIDE), cx]
        return copy(piece, piece, zsend.at[a, d - 1], zrecv.at[a, d - 1], (s, i))

    def slab(a, h, phase, c, part):
        zs = pl.ds(2 * h, 2) if part is None else 2 * h + part
        if phase == 0:
            return w.at[a, cy, zs, c] if h == 0 else w.at[a, c, zs, cx]
        return w.at[a, c, zs] if h == 0 else w.at[a, :, zs, c]

    def ring(a, h, phase, kind, arrival=False):
        along_x = phase == h
        me = cx if along_x else cy
        plus, minus = lax.rem(me + 1, SIDE), lax.rem(me + SIDE - 1, SIDE)
        across = lax.rem(me + 2, SIDE)
        part = None if kind < 2 else kind - 2
        if arrival:
            held = (minus, plus, across, across)[kind]
        else:
            held = (me, me, minus, plus)[kind]
        goes = plus if kind % 2 == 0 else minus
        to = at(cy, cz, goes) if along_x else at(goes, cz, cx)
        piece = slab(a, h, phase, held, part)
        sems = (a, h, phase, kind)
        return copy(piece, piece, rsend.at[sems], rrecv.at[sems], (s, to))

    def init_copy(m, c):
        return copy(
            grx.at[m, 0, c], grx.at[m, 1, c], isend.at[m, c], grecv.at[m, 1, c], (s, before)
        )

    def grad_copy(m, c, j):
        to = (s - 1, i) if j == 0 else (s - 1, before)
        return copy(out.at[m, c], grx.at[m, j, c], gsend.at[m, j, c], grecv.at[m, j, c], to)

    def skip_copy(m):
        return copy(out.at[m], skip.at[m], ssend.at[m], srecv.at[m], (mirror_s, i))

    def dq_copy(m):
        return copy(dqnext.at[m], dqrx.at[m], dsend.at[m], drecv.at[m], (s, after))

    for n in range(5):
        local_copy(n).start()

    @pl.when(s == top)
    def _():
        local_copy(5).start()


    barrier = pltpu.get_barrier_semaphore()

    def greet(section, seq):
        pl.semaphore_signal(barrier, inc=1, device_id=(section, seq), device_id_type=MESH)

    greet(s, after)
    greet(s, before)
    greet(mirror_s, i)
    for d in range(1, SIDE):
        greet(s, at(cy, lax.rem(cz + d, SIDE), cx))
        greet(s, at(cy, cz, lax.rem(cx + d, SIDE)))
    for d in (1, SIDE - 1):
        greet(s, at(lax.rem(cy + d, SIDE), cz, cx))
        greet(s, lax.rem(i + d * SIDE + (blocks - SIDE * SIDE if d > 1 else 0), blocks))

    @pl.when(s > 0)
    def _():
        greet(s - 1, i)
        greet(s - 1, before)

    @pl.when(s < top)
    def _():
        greet(s + 1, i)
        greet(s + 1, after)

    @pl.when(s > 1)
    def _():
        greet(s - 2, i)

    @pl.when(s < top - 1)
    def _():
        greet(s + 2, i)

    @pl.when((s == 0) | (s == top))
    def _():
        pl.semaphore_wait(barrier, 16)

    @pl.when((s == 1) | (s == top - 1))
    def _():
        pl.semaphore_wait(barrier, 18)

    @pl.when((s > 1) & (s < top - 1))
    def _():
        pl.semaphore_wait(barrier, 19)


    row = lax.broadcasted_iota(jnp.int32, (ROWS, 2 * ROWS), 0)
    col = lax.broadcasted_iota(jnp.int32, (ROWS, 2 * ROWS), 1)
    no_next = jnp.where(i == blocks - 1, 2 * ROWS, 0)
    allowed = ((col < ROWS) & (row <= col)) | ((col >= ROWS) & (row > col - ROWS + no_next))
    bias[...] = jnp.where(allowed, 0.0, -1e30)

    def each_head(body):
        for h in range(HEADS):
            body(h, slice(h * HEAD, (h + 1) * HEAD))

    def soft_in(m):
        @pl.when(cx < SIDE - 1)
        def _():
            query_copy(m).wait_recv()

        def head(h, cols):
            keys = kv[m, :, cols]
            queries = jnp.concatenate([qv[m, :, cols], qnext[m, :, cols]], 0)
            score = dot(keys, queries, NT) * scale + bias[...]
            high = jnp.maximum(jnp.max(score, axis=0, keepdims=True), -1e29)
            e = jnp.exp(score - high)
            total = jnp.sum(e, axis=0, keepdims=True)
            weight[m, h] = e
            one = slice(h, h + 1)
            stat[m, 0, 0, one] = high[:, :ROWS]
            stat[m, 1, 0, one] = high[:, ROWS:]
            stat[m, 0, 1, one] = total[:, :ROWS]
            stat[m, 1, 1, one] = total[:, ROWS:]
            kt[m, cols] = keys.T

        each_head(head)
        for side in range(2):
            stat_copy(m, side).start()

    def soft_out(m):
        for side in range(2):
            stat_copy(m, 1 - side).wait_recv()
            here, there = stat[m, side, 0], statrx[m, side, 0]
            high = jnp.maximum(here, there)
            mine = jnp.exp(here - high)
            total = stat[m, side, 1] * mine + statrx[m, side, 1] * jnp.exp(there - high)
            factor[side] = mine / total

        def head(h, cols):
            one = slice(h, h + 1)
            part = jnp.concatenate([factor[0, one], factor[1, one]], 1)
            prob[m, h] = (weight[m, h] * part).astype(BF16)

        each_head(head)

    def values():
        @pl.when(s >= half)
        def _():
            mirror_copy().wait_recv()
            xh[...] = (xv[...].astype(F32) + xmirror[...].astype(F32)).astype(BF16)

        @pl.when(s < half)
        def _():
            xh[...] = xv[...]

        def columns(c, carry):
            cols = pl.ds(pl.multiple_of(c * step, step), step)
            part = w[1, :, :, :, :, cols].reshape(width, step)
            result = dot(xh[...].reshape(2 * ROWS, width), part).astype(BF16)
            vals[:, :, cols] = result.reshape(2, ROWS, step)
            return carry

        lax.fori_loop(0, CHUNKS, columns, 0)

    def chain_in(m):
        acc[...] = jnp.zeros_like(acc)

        @pl.when((s < top) & (lax.rem(s, 2) == 0))
        def _():
            for c in range(CHUNKS):
                grad_copy(m, c, 0).wait_recv()

        @pl.when((s < top) & (lax.rem(s, 2) == 1))
        def _():
            for c in range(CHUNKS):
                grad_copy(m, c, 0).wait_recv()
                init_copy(m, c).start()

        def chunk(c, carry):
            grad_copy(m, c, 1).wait_recv()
            cols = pl.ds(pl.multiple_of(c * step, step), step)
            both = jnp.concatenate([grx[m, 0, c], grx[m, 1, c]], 1)
            part = w[0, :, :, :, :, cols].reshape(width, step)
            acc[...] += dot(part, both)
            return carry

        lax.fori_loop(0, CHUNKS, chunk, 0)
        vgi[m] = acc[...].astype(BF16)

    def chain_out(m):
        for h in range(HEADS):
            rows = slice(h * HEAD, (h + 1) * HEAD)
            vg[rows] = dot(vgi[m, rows], prob[m, h], NT).astype(BF16)

        @pl.when(s < half - 1)
        def _():
            skip_copy(m).wait_recv()

        @pl.when(s == half - 1)
        def _():
            skip[m] = grx[m, 0]

        def chunk(c, carry):
            part = w[1, c].reshape(step, width)
            total = dot(part, vg[...]) + grx[m, 0, c].astype(F32) + skip[m, c].astype(F32)
            out[m, c] = total.astype(BF16)

            @pl.when(lax.rem(s, 2) == 1)
            def _():
                grad_copy(m, c, 1).start()

            @pl.when(s > 0)
            def _():
                grad_copy(m, c, 0).start()

            return carry

        lax.fori_loop(0, CHUNKS, chunk, 0)

        @pl.when(s > half)
        def _():
            skip_copy(m).start()

    def post_in(m):
        def head(h, cols):
            grad = dot(vals[m, :, cols], vgi[m, cols])
            dprob[h] = grad
            total = jnp.sum(prob[m, h].astype(F32) * grad, axis=0, keepdims=True)
            one = slice(h, h + 1)
            delta[m, 0, one] = total[:, :ROWS]
            delta[m, 1, one] = total[:, ROWS:]

        each_head(head)
        for side in range(2):
            delta_copy(m, side).start()

    def post_out(m):
        for side in range(2):
            delta_copy(m, 1 - side).wait_recv()
            factor[side] = delta[m, side] + deltarx[m, side]

        def head(h, cols):
            one = slice(h, h + 1)
            whole = jnp.concatenate([factor[0, one], factor[1, one]], 1)
            ds = (prob[m, h].astype(F32) * (dprob[h] - whole) * scale).astype(BF16)
            queries = jnp.concatenate([qv[m, :, cols], qnext[m, :, cols]], 0)
            dk[0, m, :, cols] = dot(ds, queries).astype(BF16)
            both = dot(kt[m, cols], ds)
            dqown[m, cols] = both[:, :ROWS]
            dqnext[m, cols] = both[:, ROWS:].astype(BF16)

        each_head(head)
        dq_copy(m).start()


    @pl.when(s < top - 1)
    def _():
        pl.semaphore_wait(go_z, 1)

    @pl.when(cx == 0)
    def _():
        for j in range(1, SIDE):
            edge_out(j).start()
        edge_over(True, False).start()

    @pl.when(cx > 0)
    def _():
        for m in range(2):
            query_copy(m).start()

    for a in range(2):
        for d in range(1, SIDE):
            z_copy(a, d).start()

    for n in range(5):
        local_copy(n).wait()

    @pl.when(cx > 0)
    def _():
        edge_out(0).wait_recv()

    @pl.when((cx > 0) & (cx < SIDE - 1))
    def _():
        edge_over(False, False).start()

    @pl.when(cx == SIDE - 1)
    def _():
        edge_over(False, True).start()

    @pl.when(s == top)
    def _():
        local_copy(5).wait()
        for m in range(2):
            for c in range(CHUNKS):
                grx[m, 0, c] = ogv[m, :, c * step:(c + 1) * step].T
                init_copy(m, c).start()

    @pl.when(s >= half)
    def _():
        skip[...] = jnp.zeros_like(skip)

    for a in range(2):
        for d in range(1, SIDE):
            z_arrival(a, d).wait_recv()
        for h in range(2):
            for kind in range(2):
                ring(a, h, 0, kind).start()

    @pl.when(s > 1)
    def _():
        pl.semaphore_signal(go_z, inc=1, device_id=(s - 2, i), device_id_type=MESH)

    @pl.when(s < half)
    def _():
        mirror_copy().start()

    @pl.when(cx < SIDE - 1)
    def _():
        edge_over(False, False).wait_recv()
        edge_in().start()

    def relay(a, phase):
        for h in range(2):
            for kind in range(2):
                ring(a, h, phase, kind, True).wait_recv()
                ring(a, h, phase, kind + 2).start()

    def settle(a, phase):
        for h in range(2):
            for kind in range(2, 4):
                ring(a, h, phase, kind, True).wait_recv()

    def second():
        for a in range(2):
            settle(a, 0)
            for h in range(2):
                for kind in range(2):
                    ring(a, h, 1, kind).start()

    def each_micro(body):
        def turn(m, carry):
            body(m)
            return carry

        lax.fori_loop(0, 2, turn, 0)

    odd = lax.rem(s, 2) == 1
    for a in range(2):
        relay(a, 0)

    @pl.when(odd)
    def _():
        second()

    @pl.when(cx == SIDE - 1)
    def _():
        for j in range(SIDE):
            edge_arrival(j).wait_recv()

    each_micro(soft_in)

    @pl.when(odd)
    def _():
        for a in range(2):
            relay(a, 1)
        pl.semaphore_signal(go_r, inc=1, device_id=(s - 1, i), device_id_type=MESH)

    each_micro(soft_out)

    @pl.when(jnp.logical_not(odd))
    def _():
        pl.semaphore_wait(go_r, 1)
        second()
        for a in range(2):
            relay(a, 1)

    settle(0, 1)
    settle(1, 1)

    def turn(t, carry):
        m = lax.rem(t, 2)
        post = ((t < 2) & (s == 0)) | ((t >= 2) & (s > 0))

        @pl.when(((t == 0) & (s < half)) | ((t == 2) & (s >= half)))
        def _():
            values()

        @pl.when(t < 2)
        def _():
            chain_in(m)

        @pl.when(post)
        def _():
            post_in(m)

        @pl.when(t < 2)
        def _():
            chain_out(m)

        @pl.when(post)
        def _():
            post_out(m)

        return carry

    lax.fori_loop(0, 4, turn, 0)

    for m in range(2):
        for c in range(CHUNKS):
            sg[0, m, :, c * step:(c + 1) * step] = out[m, c].T
    for m in range(2):
        dq_copy(m).wait_recv()
        for c in range(CHUNKS):
            rows = slice(c * step, (c + 1) * step)
            dq[0, m, :, rows] = (dqown[m, rows] + dqrx[m, rows].astype(F32)).T.astype(BF16)


    @pl.when(cx == 0)
    def _():
        for j in range(1, SIDE):
            edge_out(j).wait_send()

    @pl.when(cx > 0)
    def _():
        for m in range(2):
            query_copy(m).wait_send()

    edge_over(False, False).wait_send()

    @pl.when(cx < SIDE - 1)
    def _():
        edge_in().wait_send()

    for m in range(2):
        dq_copy(m).wait_send()
        for side in range(2):
            stat_copy(m, side).wait_send()
            delta_copy(m, side).wait_send()
    for a in range(2):
        for d in range(1, SIDE):
            z_copy(a, d).wait_send()
        for h in range(2):
            for phase in range(2):
                for kind in range(4):
                    ring(a, h, phase, kind).wait_send()

    @pl.when(s < half)
    def _():
        mirror_copy().wait_send()

    @pl.when(odd)
    def _():
        for m in range(2):
            for c in range(CHUNKS):
                init_copy(m, c).wait_send()
                grad_copy(m, c, 1).wait_send()

    @pl.when(s > 0)
    def _():
        for m in range(2):
            for c in range(CHUNKS):
                grad_copy(m, c, 0).wait_send()

    @pl.when(s > half)
    def _():
        for m in range(2):
            skip_copy(m).wait_send()


def per_device(x_saved, queries, keys, value_weight, out_weight, out_grad):
    sections = lax.axis_size("section")
    blocks = lax.axis_size("seq")
    micro, rows, width = out_grad.shape
    shape = jax.ShapeDtypeStruct((1, micro, rows, width), BF16)
    step = width // CHUNKS
    vmem = pl.BlockSpec(memory_space=pltpu.VMEM)
    hbm = pl.BlockSpec(memory_space=pltpu.HBM)
    dma = pltpu.SemaphoreType.DMA
    block = pltpu.VMEM((micro, rows, width), BF16)
    turned = pltpu.VMEM((micro, width, rows), BF16)
    chunks = pltpu.VMEM((micro, CHUNKS, step, rows), BF16)
    side_rows = pltpu.VMEM((micro, 2, HEADS, rows), F32)
    return pl.pallas_call(
        functools.partial(kernel, sections, blocks, width),
        out_shape=(shape, shape, shape),
        in_specs=[hbm] * 6,
        out_specs=(vmem,) * 3,
        scratch_shapes=[
            pltpu.VMEM((2, SIDE, SIDE, SIDE, width // blocks, width), BF16),
            block,
            block,
            block,
            block,
            block,
            turned,
            block,
            block,
            block,
            pltpu.VMEM((micro, HEADS, rows, 2 * rows), F32),
            pltpu.VMEM((micro, HEADS, rows, 2 * rows), BF16),
            pltpu.VMEM((micro, 2, CHUNKS, step, rows), BF16),
            chunks,
            chunks,
            pltpu.VMEM((width, 2 * rows), F32),
            pltpu.VMEM((micro, width, 2 * rows), BF16),
            pltpu.VMEM((width, rows), BF16),
            pltpu.VMEM((micro, 2, 2, HEADS, rows), F32),
            pltpu.VMEM((micro, 2, 2, HEADS, rows), F32),
            pltpu.VMEM((2, HEADS, rows), F32),
            pltpu.VMEM((rows, 2 * rows), F32),
            pltpu.VMEM((HEADS, rows, 2 * rows), F32),
            side_rows,
            side_rows,
            pltpu.VMEM((micro, width, rows), F32),
            turned,
            turned,
            pltpu.VMEM((micro, rows // SIDE, width), BF16),
            pltpu.VMEM((micro, rows // SIDE, width), BF16),
            dma((6,)),
            dma((2,)), dma((2,)),
            dma((SIDE,)), dma((1,)),
            dma((1,)), dma((1,)),
            dma((1,)), dma((SIDE,)),
            dma((2, 2)), dma((2, 2)),
            dma((1,)), dma((1,)),
            dma((2, 3)), dma((2, 3)),
            dma((2, 2, 2, 4)), dma((2, 2, 2, 4)),
            dma((2, CHUNKS)),
            dma((2, 2, CHUNKS)), dma((2, 2, CHUNKS)),
            dma((2,)), dma((2,)),
            dma((2, 2)), dma((2, 2)),
            dma((2,)), dma((2,)),
            pltpu.SemaphoreType.REGULAR,
            pltpu.SemaphoreType.REGULAR,
        ],
        compiler_params=pltpu.CompilerParams(
            collective_id=0, has_side_effects=True, vmem_limit_bytes=60 * 2**20
        ),
        cost_estimate=pl.CostEstimate(flops=4 * 10**9, bytes_accessed=8 * 2**20, transcendentals=2**19),
        name="backward",
    )(x_saved, queries, keys, value_weight, out_weight, out_grad)


def solution(mesh):
    rows = P("section", None, "seq", None)
    weights = P("section", "seq", None)
    return jax.shard_map(
        per_device,
        mesh=mesh,
        in_specs=(rows, rows, rows, weights, weights, P(None, "seq", None)),
        out_specs=(rows, rows, rows),
        check_vma=False,
    )
```

time: 1010 us -> 165 us (0.16)
  the two profiles are of different devices: /device:TPU:6 before, /device:TPU:1 now
where the time goes in v1:
time: 165 us
  Pallas kernels  160 us (97%)
  local copies, waits for them, and re-layouts  3.95 us (2%)
    pallas_call x1, Pallas kernels, per_device(): pl.pallas_call(functools.partial(kernel, sections, blocks, width), out_sh...  160 us
    unnamed x7, local copies, waits for them, and re-layouts  3.95 us

profile of v1, /device:TPU:1, one launch (start us, length us, event | category | flops | bytes accessed | tf_op | source)
XLA Modules:
  0.0 164.8 jit_solution(1284299098853078742)
XLA Ops:
  0.6 160.2 %backward.1 = (bf16[1,2,128,1024]{3,2,1,0:T(8,128)(2,1)}, bf16[1,2,128,1024]{3,2,1,0:T(8,128)(2,1)}, bf16[1,2,128,1024]{3,2,1,0:T(8,128)(2,1)}) custom-call(bf16[1,2,128,1024]{3,2,1,0:T(8,128)(2,1)} %x.1, bf16[1,2,128,1024]{3,2,1,0:T(8,128)(2,1)} %q.1, bf16[1,2,128,1024]{3,2,1,0:T(8,128)(2,1)} %k.1, bf16[1,16,1024]{2,1,0:T(8,128)(2,1)} %wv.1, ...), custom_call_target="tpu_custom_call" | custom-call | flops 4000000000 | bytes 8388608 | tf_op jit(solution)/shard_map/backward/pallas_call | solution.py:596
  160.8 0.0 copy-start.1
  160.8 1.9 %copy.12 = bf16[1,2,128,1024]{3,2,1,0:T(8,128)(2,1)} copy(bf16[1,2,128,1024]{3,2,1,0:T(8,128)(2,1)} %get-tuple-element.6) | data formatting | bytes 1048576
  162.8 0.0 copy-done.1
  162.8 0.0 copy-start
  162.8 0.8 copy.13
  163.6 0.4 copy-done
  164.0 0.8 copy.14
Async XLA Ops:
  160.8 1.9 %copy-start.1 = (bf16[1,2,128,1024]{3,2,1,0:T(8,128)(2,1)S(1)}, bf16[1,2,128,1024]{3,2,1,0:T(8,128)(2,1)}, u32[]{:S(2)}) copy-start(bf16[1,2,128,1024]{3,2,1,0:T(8,128)(2,1)} %get-tuple-element.7) | copy-start | bytes 1572868
  162.8 1.2 copy-start

commit v2 on v1

--- a/solution.py
+++ b/solution.py
@@ -29,9 +29,9 @@
     x, q, k, wv, wo, og,
     sg, dq, dk,
     w, qv, kv, xv, ogv, qnext, kt, vals, xh, xmirror, weight, prob, grx, out, skip, acc, vgi, vg,
-    stat, statrx, factor, bias, dprob, delta, deltarx, dqown, dqnext, dqrx, pass1, pass2,
+    stat, statrx, factor, bias, dprob, delta, deltarx, dqown, dqnext, dqrx, pass1, pass2, pass3, pass4,
     lsem, qsend, qrecv, e1send, e1recv, e2send, e2recv, e3send, e3recv, tsend, trecv, msend, mrecv, zsend, zrecv, rsend, rrecv, isend,
-    gsend, grecv, ssend, srecv, esend, erecv, dsend, drecv, go_z, go_r,
+    gsend, grecv, ssend, srecv, esend, erecv, dsend, drecv, f1send, f1recv, f2send, f2recv, f3send, f3recv, go_z, go_r,
 ):
     s = lax.axis_index("section")
     i = lax.axis_index("seq")
@@ -121,12 +121,15 @@
             return w.at[a, cy, zs, c] if h == 0 else w.at[a, c, zs, cx]
         return w.at[a, c, zs] if h == 0 else w.at[a, :, zs, c]
 
+    def kinds(h, phase):
+        return (2,) if phase == h else (2, 3)
+
     def ring(a, h, phase, kind, arrival=False):
         along_x = phase == h
         me = cx if along_x else cy
         plus, minus = lax.rem(me + 1, SIDE), lax.rem(me + SIDE - 1, SIDE)
         across = lax.rem(me + 2, SIDE)
-        part = None if kind < 2 else kind - 2
+        part = None if kind < 2 or along_x else kind - 2
         if arrival:
             held = (minus, plus, across, across)[kind]
         else:
@@ -152,6 +155,30 @@
     def dq_copy(m):
         return copy(dqnext.at[m], dqrx.at[m], dsend.at[m], drecv.at[m], (s, after))
 
+
+    ahead = lax.rem(i + SIDE, blocks)
+
+    def dq_part(ref, m, j):
+        return ref.at[m, pl.ds(j * step, step)]
+
+    def dq_out(m, j):
+        to = i - SIDE + 1 + j
+        return copy(dq_part(dqnext, m, j), pass3.at[m], f1send.at[m, j], f1recv.at[m], (s, to))
+
+    def dq_over(m, first, last):
+        src = dq_part(dqnext, m, SIDE - 1) if first else pass3.at[m]
+        if last:
+            return copy(src, dq_part(dqrx, m, 0), f2send.at[m], f3recv.at[m, 0], (s, ahead))
+        return copy(src, pass4.at[m], f2send.at[m], f2recv.at[m], (s, ahead))
+
+    def dq_in(m):
+        rows = pl.ds(pl.multiple_of(cx * step, step), step)
+        return copy(pass4.at[m], dqrx.at[m, rows], f3send.at[m], f3recv.at[m, cx], (s, i - cx))
+
+    def dq_arrival(m, j):
+        part = dq_part(dqrx, m, j)
+        return copy(part, part, f3send.at[m], f3recv.at[m, j], (s, i))
+
     for n in range(5):
         local_copy(n).start()
 
@@ -193,17 +220,9 @@
     def _():
         greet(s + 2, i)
 
-    @pl.when((s == 0) | (s == top))
-    def _():
-        pl.semaphore_wait(barrier, 16)
-
-    @pl.when((s == 1) | (s == top - 1))
-    def _():
-        pl.semaphore_wait(barrier, 18)
-
-    @pl.when((s > 1) & (s < top - 1))
-    def _():
-        pl.semaphore_wait(barrier, 19)
+    odd = lax.rem(s, 2) == 1
+    peers = 13 + lax.div(s + 6, sections) + lax.div(2 * top - 1 - s, sections) + 2 * lax.div(s + top, sections) + 2 * lax.div(2 * top - s, sections)
+    pl.semaphore_wait(barrier, peers)
 
 
     row = lax.broadcasted_iota(jnp.int32, (ROWS, 2 * ROWS), 0)
@@ -363,54 +382,87 @@
             dqnext[m, cols] = both[:, ROWS:].astype(BF16)
 
         each_head(head)
-        dq_copy(m).start()
-
+
+        @pl.when(cx < SIDE - 1)
+        def _():
+            dq_copy(m).start()
+
+        @pl.when(cx == SIDE - 1)
+        def _():
+            for j in range(SIDE - 1):
+                dq_out(m, j).start()
+            dq_over(m, True, False).start()
+
+
+    def relay(a, phase):
+        for h in range(2):
+            for kind in range(2):
+                ring(a, h, phase, kind, True).wait_recv()
+                if kind + 2 in kinds(h, phase):
+                    ring(a, h, phase, kind + 2).start()
+
+    def settle(a, phase):
+        for h in range(2):
+            for kind in kinds(h, phase):
+                ring(a, h, phase, kind, True).wait_recv()
+
+    def second():
+        for a in range(2):
+            settle(a, 0)
+            for h in range(2):
+                for kind in range(2):
+                    ring(a, h, 1, kind).start()
+
+    def each_micro(body):
+        def turn(m, carry):
+            body(m)
+            return carry
+
+        lax.fori_loop(0, 2, turn, 0)
+
+    def start_queries():
+        @pl.when(cx == 0)
+        def _():
+            for j in range(1, SIDE):
+                edge_out(j).start()
+            edge_over(True, False).start()
+
+        @pl.when(cx > 0)
+        def _():
+            for m in range(2):
+                query_copy(m).start()
+
+    def edge_first():
+        @pl.when(cx > 0)
+        def _():
+            edge_out(0).wait_recv()
+
+        @pl.when((cx > 0) & (cx < SIDE - 1))
+        def _():
+            edge_over(False, False).start()
+
+        @pl.when(cx == SIDE - 1)
+        def _():
+            edge_over(False, True).start()
+
+    def edge_second():
+        @pl.when(cx < SIDE - 1)
+        def _():
+            edge_over(False, False).wait_recv()
+            edge_in().start()
 
     @pl.when(s < top - 1)
     def _():
         pl.semaphore_wait(go_z, 1)
-
-    @pl.when(cx == 0)
-    def _():
-        for j in range(1, SIDE):
-            edge_out(j).start()
-        edge_over(True, False).start()
-
-    @pl.when(cx > 0)
-    def _():
-        for m in range(2):
-            query_copy(m).start()
 
     for a in range(2):
         for d in range(1, SIDE):
             z_copy(a, d).start()
 
+    start_queries()
+
     for n in range(5):
         local_copy(n).wait()
-
-    @pl.when(cx > 0)
-    def _():
-        edge_out(0).wait_recv()
-
-    @pl.when((cx > 0) & (cx < SIDE - 1))
-    def _():
-        edge_over(False, False).start()
-
-    @pl.when(cx == SIDE - 1)
-    def _():
-        edge_over(False, True).start()
-
-    @pl.when(s == top)
-    def _():
-        local_copy(5).wait()
-        for m in range(2):
-            for c in range(CHUNKS):
-                grx[m, 0, c] = ogv[m, :, c * step:(c + 1) * step].T
-                init_copy(m, c).start()
-
-    @pl.when(s >= half)
-    def _():
-        skip[...] = jnp.zeros_like(skip)
 
     for a in range(2):
         for d in range(1, SIDE):
@@ -427,56 +479,38 @@
     def _():
         mirror_copy().start()
 
-    @pl.when(cx < SIDE - 1)
-    def _():
-        edge_over(False, False).wait_recv()
-        edge_in().start()
-
-    def relay(a, phase):
-        for h in range(2):
-            for kind in range(2):
-                ring(a, h, phase, kind, True).wait_recv()
-                ring(a, h, phase, kind + 2).start()
-
-    def settle(a, phase):
-        for h in range(2):
-            for kind in range(2, 4):
-                ring(a, h, phase, kind, True).wait_recv()
-
-    def second():
-        for a in range(2):
-            settle(a, 0)
-            for h in range(2):
-                for kind in range(2):
-                    ring(a, h, 1, kind).start()
-
-    def each_micro(body):
-        def turn(m, carry):
-            body(m)
-            return carry
-
-        lax.fori_loop(0, 2, turn, 0)
-
-    odd = lax.rem(s, 2) == 1
+    edge_first()
+
     for a in range(2):
         relay(a, 0)
 
+    edge_second()
+
     @pl.when(odd)
     def _():
         second()
-
-    @pl.when(cx == SIDE - 1)
-    def _():
-        for j in range(SIDE):
-            edge_arrival(j).wait_recv()
-
-    each_micro(soft_in)
-
-    @pl.when(odd)
-    def _():
         for a in range(2):
             relay(a, 1)
         pl.semaphore_signal(go_r, inc=1, device_id=(s - 1, i), device_id_type=MESH)
+
+    @pl.when(s == top)
+    def _():
+        local_copy(5).wait()
+        for m in range(2):
+            for c in range(CHUNKS):
+                grx[m, 0, c] = ogv[m, :, c * step:(c + 1) * step].T
+                init_copy(m, c).start()
+
+    @pl.when(s >= half)
+    def _():
+        skip[...] = jnp.zeros_like(skip)
+
+    @pl.when(cx == SIDE - 1)
+    def _():
+        for j in range(SIDE):
+            edge_arrival(j).wait_recv()
+
+    each_micro(soft_in)
 
     each_micro(soft_out)
 
@@ -519,10 +553,37 @@
     lax.fori_loop(0, 4, turn, 0)
 
     for m in range(2):
+        @pl.when(cx < SIDE - 1)
+        def _():
+            dq_out(m, 0).wait_recv()
+
+        @pl.when((cx > 0) & (cx < SIDE - 1))
+        def _():
+            dq_over(m, False, False).start()
+
+        @pl.when(cx == 0)
+        def _():
+            dq_over(m, False, True).start()
+
+    for m in range(2):
+        @pl.when(cx > 0)
+        def _():
+            dq_over(m, False, False).wait_recv()
+            dq_in(m).start()
+
+    for m in range(2):
         for c in range(CHUNKS):
             sg[0, m, :, c * step:(c + 1) * step] = out[m, c].T
     for m in range(2):
-        dq_copy(m).wait_recv()
+        @pl.when(cx > 0)
+        def _():
+            dq_copy(m).wait_recv()
+
+        @pl.when(cx == 0)
+        def _():
+            for j in range(SIDE):
+                dq_arrival(m, j).wait_recv()
+
         for c in range(CHUNKS):
             rows = slice(c * step, (c + 1) * step)
             dq[0, m, :, rows] = (dqown[m, rows] + dqrx[m, rows].astype(F32)).T.astype(BF16)
@@ -545,7 +606,21 @@
         edge_in().wait_send()
 
     for m in range(2):
-        dq_copy(m).wait_send()
+        @pl.when(cx < SIDE - 1)
+        def _():
+            dq_copy(m).wait_send()
+
+        @pl.when(cx == SIDE - 1)
+        def _():
+            for j in range(SIDE - 1):
+                dq_out(m, j).wait_send()
+
+        dq_over(m, False, False).wait_send()
+
+        @pl.when(cx > 0)
+        def _():
+            dq_in(m).wait_send()
+
         for side in range(2):
             stat_copy(m, side).wait_send()
             delta_copy(m, side).wait_send()
@@ -554,7 +629,7 @@
             z_copy(a, d).wait_send()
         for h in range(2):
             for phase in range(2):
-                for kind in range(4):
+                for kind in (0, 1) + kinds(h, phase):
                     ring(a, h, phase, kind).wait_send()
 
     @pl.when(s < half)
@@ -629,6 +704,8 @@
             turned,
             pltpu.VMEM((micro, rows // SIDE, width), BF16),
             pltpu.VMEM((micro, rows // SIDE, width), BF16),
+            pltpu.VMEM((micro, step, rows), BF16),
+            pltpu.VMEM((micro, step, rows), BF16),
             dma((6,)),
             dma((2,)), dma((2,)),
             dma((SIDE,)), dma((1,)),
@@ -643,6 +720,9 @@
             dma((2,)), dma((2,)),
             dma((2, 2)), dma((2, 2)),
             dma((2,)), dma((2,)),
+            dma((2, SIDE)), dma((2,)),
+            dma((2,)), dma((2,)),
+            dma((2,)), dma((2, SIDE)),
             pltpu.SemaphoreType.REGULAR,
             pltpu.SemaphoreType.REGULAR,
         ],

time: 165 us -> 166 us (level)
  no operation moved by 1% of the time
where the time goes in v2:
time: 166 us
  Pallas kernels  161 us (97%)
  local copies, waits for them, and re-layouts  3.95 us (2%)
    pallas_call x1, Pallas kernels, per_device(): pl.pallas_call(functools.partial(kernel, sections, blocks, width), out_sh...  161 us
    unnamed x7, local copies, waits for them, and re-layouts  3.95 us

profile of v2, /device:TPU:1, one launch (start us, length us, event | category | flops | bytes accessed | tf_op | source)
XLA Modules:
  0.0 166.0 jit_solution(6661241049716557746)
XLA Ops:
  0.6 161.4 %backward.1 = (bf16[1,2,128,1024]{3,2,1,0:T(8,128)(2,1)}, bf16[1,2,128,1024]{3,2,1,0:T(8,128)(2,1)}, bf16[1,2,128,1024]{3,2,1,0:T(8,128)(2,1)}) custom-call(bf16[1,2,128,1024]{3,2,1,0:T(8,128)(2,1)} %x.1, bf16[1,2,128,1024]{3,2,1,0:T(8,128)(2,1)} %q.1, bf16[1,2,128,1024]{3,2,1,0:T(8,128)(2,1)} %k.1, bf16[1,16,1024]{2,1,0:T(8,128)(2,1)} %wv.1, ...), custom_call_target="tpu_custom_call" | custom-call | flops 4000000000 | bytes 8388608 | tf_op jit(solution)/shard_map/backward/pallas_call | solution.py:671
  162.0 0.0 copy-start.1
  162.0 1.9 %copy.12 = bf16[1,2,128,1024]{3,2,1,0:T(8,128)(2,1)} copy(bf16[1,2,128,1024]{3,2,1,0:T(8,128)(2,1)} %get-tuple-element.6) | data formatting | bytes 1048576
  164.0 0.0 copy-done.1
  164.0 0.0 copy-start
  164.0 0.8 copy.13
  164.8 0.4 copy-done
  165.2 0.8 copy.14
Async XLA Ops:
  162.0 1.9 %copy-start.1 = (bf16[1,2,128,1024]{3,2,1,0:T(8,128)(2,1)S(1)}, bf16[1,2,128,1024]{3,2,1,0:T(8,128)(2,1)}, u32[]{:S(2)}) copy-start(bf16[1,2,128,1024]{3,2,1,0:T(8,128)(2,1)} %get-tuple-element.7) | copy-start | bytes 1572868
  164.0 1.2 copy-start

commit v3 on v2

--- a/solution.py
+++ b/solution.py
@@ -13,7 +13,7 @@
 HEAD = 128
 ROWS = 128
 SIDE = 4
-CHUNKS = 4
+CHUNKS = 2
 BF16 = jnp.bfloat16
 F32 = jnp.float32
 NN = (((1,), (0,)), ((), ()))
@@ -157,9 +157,10 @@
 
 
     ahead = lax.rem(i + SIDE, blocks)
+    fourth = width // SIDE
 
     def dq_part(ref, m, j):
-        return ref.at[m, pl.ds(j * step, step)]
+        return ref.at[m, pl.ds(j * fourth, fourth)]
 
     def dq_out(m, j):
         to = i - SIDE + 1 + j
@@ -172,7 +173,7 @@
         return copy(src, pass4.at[m], f2send.at[m], f2recv.at[m], (s, ahead))
 
     def dq_in(m):
-        rows = pl.ds(pl.multiple_of(cx * step, step), step)
+        rows = pl.ds(pl.multiple_of(cx * fourth, fourth), fourth)
         return copy(pass4.at[m], dqrx.at[m, rows], f3send.at[m], f3recv.at[m, cx], (s, i - cx))
 
     def dq_arrival(m, j):
@@ -333,7 +334,7 @@
             skip[m] = grx[m, 0]
 
         def chunk(c, carry):
-            part = w[1, c].reshape(step, width)
+            part = w[1, pl.ds(c * (SIDE // CHUNKS), SIDE // CHUNKS)].reshape(step, width)
             total = dot(part, vg[...]) + grx[m, 0, c].astype(F32) + skip[m, c].astype(F32)
             out[m, c] = total.astype(BF16)
 
@@ -475,10 +476,6 @@
     def _():
         pl.semaphore_signal(go_z, inc=1, device_id=(s - 2, i), device_id_type=MESH)
 
-    @pl.when(s < half)
-    def _():
-        mirror_copy().start()
-
     edge_first()
 
     for a in range(2):
@@ -523,6 +520,10 @@
 
     settle(0, 1)
     settle(1, 1)
+
+    @pl.when(s < half)
+    def _():
+        mirror_copy().start()
 
     def turn(t, carry):
         m = lax.rem(t, 2)
@@ -704,8 +705,8 @@
             turned,
             pltpu.VMEM((micro, rows // SIDE, width), BF16),
             pltpu.VMEM((micro, rows // SIDE, width), BF16),
-            pltpu.VMEM((micro, step, rows), BF16),
-            pltpu.VMEM((micro, step, rows), BF16),
+            pltpu.VMEM((micro, width // SIDE, rows), BF16),
+            pltpu.VMEM((micro, width // SIDE, rows), BF16),
             dma((6,)),
             dma((2,)), dma((2,)),
             dma((SIDE,)), dma((1,)),

time: 166 us -> 168 us (1.012)
  Pallas kernels: 161 us -> 163 us
    pallas_call x1, Pallas kernels: 161 us -> 163 us  [per_device(): pl.pallas_call(functools.partial(kernel, sections, blocks, width), out_sh...]
where the time goes in v3:
time: 168 us
  Pallas kernels  163 us (97%)
  local copies, waits for them, and re-layouts  3.95 us (2%)
    pallas_call x1, Pallas kernels, per_device(): pl.pallas_call(functools.partial(kernel, sections, blocks, width), out_sh...  163 us
    unnamed x7, local copies, waits for them, and re-layouts  3.95 us

profile of v3, /device:TPU:1, one launch (start us, length us, event | category | flops | bytes accessed | tf_op | source)
XLA Modules:
  0.0 167.8 jit_solution(15987364287278732298)
XLA Ops:
  0.6 163.2 %backward.1 = (bf16[1,2,128,1024]{3,2,1,0:T(8,128)(2,1)}, bf16[1,2,128,1024]{3,2,1,0:T(8,128)(2,1)}, bf16[1,2,128,1024]{3,2,1,0:T(8,128)(2,1)}) custom-call(bf16[1,2,128,1024]{3,2,1,0:T(8,128)(2,1)} %x.1, bf16[1,2,128,1024]{3,2,1,0:T(8,128)(2,1)} %q.1, bf16[1,2,128,1024]{3,2,1,0:T(8,128)(2,1)} %k.1, bf16[1,16,1024]{2,1,0:T(8,128)(2,1)} %wv.1, ...), custom_call_target="tpu_custom_call" | custom-call | flops 4000000000 | bytes 8388608 | tf_op jit(solution)/shard_map/backward/pallas_call | solution.py:672
  163.8 0.0 copy-start.1
  163.8 1.9 %copy.12 = bf16[1,2,128,1024]{3,2,1,0:T(8,128)(2,1)} copy(bf16[1,2,128,1024]{3,2,1,0:T(8,128)(2,1)} %get-tuple-element.6) | data formatting | bytes 1048576
  165.7 0.0 copy-done.1
  165.8 0.0 copy-start
  165.8 0.8 copy.13
  166.5 0.4 copy-done
  167.0 0.8 copy.14
Async XLA Ops:
  163.8 1.9 %copy-start.1 = (bf16[1,2,128,1024]{3,2,1,0:T(8,128)(2,1)S(1)}, bf16[1,2,128,1024]{3,2,1,0:T(8,128)(2,1)}, u32[]{:S(2)}) copy-start(bf16[1,2,128,1024]{3,2,1,0:T(8,128)(2,1)} %get-tuple-element.7) | copy-start | bytes 1572868
  165.8 1.2 copy-start

commit v4 on v2

--- a/solution.py
+++ b/solution.py
@@ -30,7 +30,7 @@
     sg, dq, dk,
     w, qv, kv, xv, ogv, qnext, kt, vals, xh, xmirror, weight, prob, grx, out, skip, acc, vgi, vg,
     stat, statrx, factor, bias, dprob, delta, deltarx, dqown, dqnext, dqrx, pass1, pass2, pass3, pass4,
-    lsem, qsend, qrecv, e1send, e1recv, e2send, e2recv, e3send, e3recv, tsend, trecv, msend, mrecv, zsend, zrecv, rsend, rrecv, isend,
+    lsem, wsem, qsend, qrecv, e1send, e1recv, e2send, e2recv, e3send, e3recv, tsend, trecv, msend, mrecv, zsend, zrecv, rsend, rrecv, isend,
     gsend, grecv, ssend, srecv, esend, erecv, dsend, drecv, f1send, f1recv, f2send, f2recv, f3send, f3recv, go_z, go_r,
 ):
     s = lax.axis_index("section")
@@ -44,6 +44,7 @@
     half = sections // 2
     mirror_s = top - s
     step = width // CHUNKS
+    per = step // HEAD
     scale = 1.0 / math.sqrt(HEAD)
 
     def at(y, z, x_):
@@ -57,11 +58,17 @@
 
 
     def local_copy(n):
-        src, dst = (
-            (q.at[0], qv), (k.at[0], kv), (wo.at[0], w.at[0, cy, cz, cx]),
-            (wv.at[0], w.at[1, cy, cz, cx]), (x.at[0], xv), (og, ogv),
-        )[n]
+        src, dst = ((q.at[0], qv), (k.at[0], kv), (x.at[0], xv), (og, ogv))[n]
         return pltpu.make_async_copy(src, dst, lsem.at[n])
+
+
+    def shard_copy(a, b):
+        src = (wo if a == 0 else wv).at[0, :, pl.ds(b * HEAD, HEAD)]
+        return pltpu.make_async_copy(src, w.at[a, cy, cz, cx, b], wsem.at[a, b])
+
+    def columns_of(part, first, count, rows):
+        blocks_of = [part(first + n).reshape(rows, HEAD) for n in range(count)]
+        return jnp.concatenate(blocks_of, 1)
 
     def query_copy(m):
         return copy(q.at[0, m], qnext.at[m], qsend.at[m], qrecv.at[m], (s, before))
@@ -108,8 +115,8 @@
 
     def z_copy(a, d):
         to = at(cy, lax.rem(cz + d, SIDE), cx)
-        src = (wo if a == 0 else wv).at[0]
-        return copy(src, w.at[a, cy, cz, cx], zsend.at[a, d - 1], zrecv.at[a, d - 1], (s, to))
+        piece = w.at[a, cy, cz, cx]
+        return copy(piece, piece, zsend.at[a, d - 1], zrecv.at[a, d - 1], (s, to))
 
     def z_arrival(a, d):
         piece = w.at[a, cy, lax.rem(cz + SIDE - d, SIDE), cx]
@@ -179,12 +186,15 @@
         part = dq_part(dqrx, m, j)
         return copy(part, part, f3send.at[m], f3recv.at[m, j], (s, i))
 
-    for n in range(5):
+    for a in range(2):
+        for b in range(width // HEAD):
+            shard_copy(a, b).start()
+    for n in range(3):
         local_copy(n).start()
 
     @pl.when(s == top)
     def _():
-        local_copy(5).start()
+        local_copy(3).start()
 
 
     barrier = pltpu.get_barrier_semaphore()
@@ -271,7 +281,9 @@
         def head(h, cols):
             one = slice(h, h + 1)
             part = jnp.concatenate([factor[0, one], factor[1, one]], 1)
-            prob[m, h] = (weight[m, h] * part).astype(BF16)
+            p = (weight[m, h] * part).astype(BF16)
+            prob[m, h, 0] = p[:, :ROWS]
+            prob[m, h, 1] = p[:, ROWS:]
 
         each_head(head)
 
@@ -286,10 +298,12 @@
             xh[...] = xv[...]
 
         def columns(c, carry):
-            cols = pl.ds(pl.multiple_of(c * step, step), step)
-            part = w[1, :, :, :, :, cols].reshape(width, step)
+            part = columns_of(lambda b: w[1, :, :, :, b], c * per, per, width)
             result = dot(xh[...].reshape(2 * ROWS, width), part).astype(BF16)
-            vals[:, :, cols] = result.reshape(2, ROWS, step)
+            for m in range(2):
+                for u in range(per):
+                    block = result[m * ROWS:(m + 1) * ROWS, u * HEAD:(u + 1) * HEAD]
+                    vals[m, c * per + u] = block
             return carry
 
         lax.fori_loop(0, CHUNKS, columns, 0)
@@ -310,19 +324,21 @@
 
         def chunk(c, carry):
             grad_copy(m, c, 1).wait_recv()
-            cols = pl.ds(pl.multiple_of(c * step, step), step)
             both = jnp.concatenate([grx[m, 0, c], grx[m, 1, c]], 1)
-            part = w[0, :, :, :, :, cols].reshape(width, step)
+            part = columns_of(lambda b: w[0, :, :, :, b], c * per, per, width)
             acc[...] += dot(part, both)
             return carry
 
         lax.fori_loop(0, CHUNKS, chunk, 0)
-        vgi[m] = acc[...].astype(BF16)
+        vgi[m, 0] = acc[:, :ROWS].astype(BF16)
+        vgi[m, 1] = acc[:, ROWS:].astype(BF16)
 
     def chain_out(m):
         for h in range(HEADS):
             rows = slice(h * HEAD, (h + 1) * HEAD)
-            vg[rows] = dot(vgi[m, rows], prob[m, h], NT).astype(BF16)
+            grad = jnp.concatenate([vgi[m, 0, rows], vgi[m, 1, rows]], 1)
+            p = jnp.concatenate([prob[m, h, 0], prob[m, h, 1]], 1)
+            vg[rows] = dot(grad, p, NT).astype(BF16)
 
         @pl.when(s < half - 1)
         def _():
@@ -333,7 +349,7 @@
             skip[m] = grx[m, 0]
 
         def chunk(c, carry):
-            part = w[1, c].reshape(step, width)
+            part = columns_of(lambda b: w[1, c, :, :, b], 0, width // HEAD, step)
             total = dot(part, vg[...]) + grx[m, 0, c].astype(F32) + skip[m, c].astype(F32)
             out[m, c] = total.astype(BF16)
 
@@ -355,9 +371,11 @@
 
     def post_in(m):
         def head(h, cols):
-            grad = dot(vals[m, :, cols], vgi[m, cols])
-            dprob[h] = grad
-            total = jnp.sum(prob[m, h].astype(F32) * grad, axis=0, keepdims=True)
+            both = jnp.concatenate([vgi[m, 0, cols], vgi[m, 1, cols]], 1)
+            grad = dot(vals[m, h], both)
+            dprob[m, h] = grad
+            p = jnp.concatenate([prob[m, h, 0], prob[m, h, 1]], 1).astype(F32)
+            total = jnp.sum(p * grad, axis=0, keepdims=True)
             one = slice(h, h + 1)
             delta[m, 0, one] = total[:, :ROWS]
             delta[m, 1, one] = total[:, ROWS:]
@@ -374,7 +392,8 @@
         def head(h, cols):
             one = slice(h, h + 1)
             whole = jnp.concatenate([factor[0, one], factor[1, one]], 1)
-            ds = (prob[m, h].astype(F32) * (dprob[h] - whole) * scale).astype(BF16)
+            p = jnp.concatenate([prob[m, h, 0], prob[m, h, 1]], 1).astype(F32)
+            ds = (p * (dprob[m, h] - whole) * scale).astype(BF16)
             queries = jnp.concatenate([qv[m, :, cols], qnext[m, :, cols]], 0)
             dk[0, m, :, cols] = dot(ds, queries).astype(BF16)
             both = dot(kt[m, cols], ds)
@@ -456,12 +475,14 @@
         pl.semaphore_wait(go_z, 1)
 
     for a in range(2):
+        for b in range(width // HEAD):
+            shard_copy(a, b).wait()
         for d in range(1, SIDE):
             z_copy(a, d).start()
 
     start_queries()
 
-    for n in range(5):
+    for n in range(3):
         local_copy(n).wait()
 
     for a in range(2):
@@ -475,10 +496,6 @@
     def _():
         pl.semaphore_signal(go_z, inc=1, device_id=(s - 2, i), device_id_type=MESH)
 
-    @pl.when(s < half)
-    def _():
-        mirror_copy().start()
-
     edge_first()
 
     for a in range(2):
@@ -495,7 +512,7 @@
 
     @pl.when(s == top)
     def _():
-        local_copy(5).wait()
+        local_copy(3).wait()
         for m in range(2):
             for c in range(CHUNKS):
                 grx[m, 0, c] = ogv[m, :, c * step:(c + 1) * step].T
@@ -524,9 +541,13 @@
     settle(0, 1)
     settle(1, 1)
 
+    @pl.when(s < half)
+    def _():
+        mirror_copy().start()
+
     def turn(t, carry):
         m = lax.rem(t, 2)
-        post = ((t < 2) & (s == 0)) | ((t >= 2) & (s > 0))
+        early = (t < 2) & (s == 0)
 
         @pl.when(((t == 0) & (s < half)) | ((t == 2) & (s >= half)))
         def _():
@@ -536,7 +557,7 @@
         def _():
             chain_in(m)
 
-        @pl.when(post)
+        @pl.when(early | ((t >= 2) & (t < 4) & (s > 0)))
         def _():
             post_in(m)
 
@@ -544,13 +565,13 @@
         def _():
             chain_out(m)
 
-        @pl.when(post)
+        @pl.when(early | ((t >= 4) & (s > 0)))
         def _():
             post_out(m)
 
         return carry
 
-    lax.fori_loop(0, 4, turn, 0)
+    lax.fori_loop(0, 6, turn, 0)
 
     for m in range(2):
         @pl.when(cx < SIDE - 1)
@@ -586,7 +607,7 @@
 
         for c in range(CHUNKS):
             rows = slice(c * step, (c + 1) * step)
-            dq[0, m, :, rows] = (dqown[m, rows] + dqrx[m, rows].astype(F32)).T.astype(BF16)
+            dq[0, m, :, rows] = (dqown[m, rows] + dqrx[m, rows].astype(F32)).astype(BF16).T
 
 
     @pl.when(cx == 0)
@@ -674,29 +695,29 @@
         in_specs=[hbm] * 6,
         out_specs=(vmem,) * 3,
         scratch_shapes=[
-            pltpu.VMEM((2, SIDE, SIDE, SIDE, width // blocks, width), BF16),
+            pltpu.VMEM((2, SIDE, SIDE, SIDE, width // HEAD, width // blocks, HEAD), BF16),
             block,
             block,
             block,
             block,
             block,
             turned,
-            block,
+            pltpu.VMEM((micro, HEADS, rows, HEAD), BF16),
             block,
             block,
             pltpu.VMEM((micro, HEADS, rows, 2 * rows), F32),
-            pltpu.VMEM((micro, HEADS, rows, 2 * rows), BF16),
+            pltpu.VMEM((micro, HEADS, 2, rows, rows), BF16),
             pltpu.VMEM((micro, 2, CHUNKS, step, rows), BF16),
             chunks,
             chunks,
             pltpu.VMEM((width, 2 * rows), F32),
-            pltpu.VMEM((micro, width, 2 * rows), BF16),
+            pltpu.VMEM((micro, 2, width, rows), BF16),
             pltpu.VMEM((width, rows), BF16),
             pltpu.VMEM((micro, 2, 2, HEADS, rows), F32),
             pltpu.VMEM((micro, 2, 2, HEADS, rows), F32),
             pltpu.VMEM((2, HEADS, rows), F32),
             pltpu.VMEM((rows, 2 * rows), F32),
-            pltpu.VMEM((HEADS, rows, 2 * rows), F32),
+            pltpu.VMEM((micro, HEADS, rows, 2 * rows), F32),
             side_rows,
             side_rows,
             pltpu.VMEM((micro, width, rows), F32),
@@ -706,7 +727,7 @@
             pltpu.VMEM((micro, rows // SIDE, width), BF16),
             pltpu.VMEM((micro, step, rows), BF16),
             pltpu.VMEM((micro, step, rows), BF16),
-            dma((6,)),
+            dma((4,)), dma((2, width // HEAD)),
             dma((2,)), dma((2,)),
             dma((SIDE,)), dma((1,)),
             dma((1,)), dma((1,)),

time: 166 us -> 164 us (0.988)
  Pallas kernels: 161 us -> 159 us
    pallas_call x1, Pallas kernels: 161 us -> 159 us  [per_device(): pl.pallas_call(functools.partial(kernel, sections, blocks, width), out_sh...]
where the time goes in v4:
time: 164 us
  Pallas kernels  159 us (97%)
  local copies, waits for them, and re-layouts  3.95 us (2%)
    pallas_call x1, Pallas kernels, per_device(): pl.pallas_call(functools.partial(kernel, sections, blocks, width), out_sh...  159 us
    unnamed x7, local copies, waits for them, and re-layouts  3.95 us

profile of v4, /device:TPU:1, one launch (start us, length us, event | category | flops | bytes accessed | tf_op | source)
XLA Modules:
  0.0 163.8 jit_solution(4402854568948814819)
XLA Ops:
  0.6 159.2 %backward.1 = (bf16[1,2,128,1024]{3,2,1,0:T(8,128)(2,1)}, bf16[1,2,128,1024]{3,2,1,0:T(8,128)(2,1)}, bf16[1,2,128,1024]{3,2,1,0:T(8,128)(2,1)}) custom-call(bf16[1,2,128,1024]{3,2,1,0:T(8,128)(2,1)} %x.1, bf16[1,2,128,1024]{3,2,1,0:T(8,128)(2,1)} %q.1, bf16[1,2,128,1024]{3,2,1,0:T(8,128)(2,1)} %k.1, bf16[1,16,1024]{2,1,0:T(8,128)(2,1)} %wv.1, ...), custom_call_target="tpu_custom_call" | custom-call | flops 4000000000 | bytes 8388608 | tf_op jit(solution)/shard_map/backward/pallas_call | solution.py:692
  159.8 0.0 copy-start.1
  159.8 1.9 %copy.12 = bf16[1,2,128,1024]{3,2,1,0:T(8,128)(2,1)} copy(bf16[1,2,128,1024]{3,2,1,0:T(8,128)(2,1)} %get-tuple-element.6) | data formatting | bytes 1048576
  161.8 0.0 copy-done.1
  161.8 0.0 copy-start
  161.8 0.8 copy.13
  162.6 0.4 copy-done
  163.0 0.8 copy.14
Async XLA Ops:
  159.8 1.9 %copy-start.1 = (bf16[1,2,128,1024]{3,2,1,0:T(8,128)(2,1)S(1)}, bf16[1,2,128,1024]{3,2,1,0:T(8,128)(2,1)}, u32[]{:S(2)}) copy-start(bf16[1,2,128,1024]{3,2,1,0:T(8,128)(2,1)} %get-tuple-element.7) | copy-start | bytes 1572868
  161.8 1.2 copy-start

commit v5 on v4

--- a/solution.py
+++ b/solution.py
@@ -548,6 +548,7 @@
     def turn(t, carry):
         m = lax.rem(t, 2)
         early = (t < 2) & (s == 0)
+        late = t - 1 - 3 * lax.div(s + top, sections)
 
         @pl.when(((t == 0) & (s < half)) | ((t == 2) & (s >= half)))
         def _():
@@ -561,13 +562,13 @@
         def _():
             post_in(m)
 
+        @pl.when(((s == 0) & (t >= 1) & (t <= 2)) | ((s > 0) & (t >= 4)))
+        def _():
+            post_out(late)
+
         @pl.when(t < 2)
         def _():
             chain_out(m)
-
-        @pl.when(early | ((t >= 4) & (s > 0)))
-        def _():
-            post_out(m)
 
         return carry
 

time: 164 us -> 165 us (level)
  no operation moved by 1% of the time
where the time goes in v5:
time: 165 us
  Pallas kernels  160 us (97%)
  local copies, waits for them, and re-layouts  3.95 us (2%)
    pallas_call x1, Pallas kernels, per_device(): pl.pallas_call(functools.partial(kernel, sections, blocks, width), out_sh...  160 us
    unnamed x7, local copies, waits for them, and re-layouts  3.95 us

profile of v5, /device:TPU:1, one launch (start us, length us, event | category | flops | bytes accessed | tf_op | source)
XLA Modules:
  0.0 164.9 jit_solution(3688350542405121373)
XLA Ops:
  0.6 160.3 %backward.1 = (bf16[1,2,128,1024]{3,2,1,0:T(8,128)(2,1)}, bf16[1,2,128,1024]{3,2,1,0:T(8,128)(2,1)}, bf16[1,2,128,1024]{3,2,1,0:T(8,128)(2,1)}) custom-call(bf16[1,2,128,1024]{3,2,1,0:T(8,128)(2,1)} %x.1, bf16[1,2,128,1024]{3,2,1,0:T(8,128)(2,1)} %q.1, bf16[1,2,128,1024]{3,2,1,0:T(8,128)(2,1)} %k.1, bf16[1,16,1024]{2,1,0:T(8,128)(2,1)} %wv.1, ...), custom_call_target="tpu_custom_call" | custom-call | flops 4000000000 | bytes 8388608 | tf_op jit(solution)/shard_map/backward/pallas_call | solution.py:693
  160.9 0.0 copy-start.1
  160.9 1.9 %copy.12 = bf16[1,2,128,1024]{3,2,1,0:T(8,128)(2,1)} copy(bf16[1,2,128,1024]{3,2,1,0:T(8,128)(2,1)} %get-tuple-element.6) | data formatting | bytes 1048576
  162.8 0.0 copy-done.1
  162.8 0.0 copy-start
  162.8 0.8 copy.13
  163.6 0.4 copy-done
  164.1 0.8 copy.14
Async XLA Ops:
  160.9 1.9 %copy-start.1 = (bf16[1,2,128,1024]{3,2,1,0:T(8,128)(2,1)S(1)}, bf16[1,2,128,1024]{3,2,1,0:T(8,128)(2,1)}, u32[]{:S(2)}) copy-start(bf16[1,2,128,1024]{3,2,1,0:T(8,128)(2,1)} %get-tuple-element.7) | copy-start | bytes 1572868
  162.8 1.2 copy-start

commit v6 on v4

--- a/solution.py
+++ b/solution.py
@@ -522,6 +522,11 @@
     def _():
         skip[...] = jnp.zeros_like(skip)
 
+    @pl.when(jnp.logical_not(odd))
+    def _():
+        pl.semaphore_wait(go_r, 1)
+        second()
+
     @pl.when(cx == SIDE - 1)
     def _():
         for j in range(SIDE):
@@ -533,8 +538,6 @@
 
     @pl.when(jnp.logical_not(odd))
     def _():
-        pl.semaphore_wait(go_r, 1)
-        second()
         for a in range(2):
             relay(a, 1)
 

time: 164 us -> 166 us (1.012)
  Pallas kernels: 159 us -> 161 us
    pallas_call x1, Pallas kernels: 159 us -> 161 us  [per_device(): pl.pallas_call(functools.partial(kernel, sections, blocks, width), out_sh...]
where the time goes in v6:
time: 166 us
  Pallas kernels  161 us (97%)
  local copies, waits for them, and re-layouts  3.95 us (2%)
    pallas_call x1, Pallas kernels, per_device(): pl.pallas_call(functools.partial(kernel, sections, blocks, width), out_sh...  161 us
    unnamed x7, local copies, waits for them, and re-layouts  3.95 us

profile of v6, /device:TPU:1, one launch (start us, length us, event | category | flops | bytes accessed | tf_op | source)
XLA Modules:
  0.0 165.5 jit_solution(6068470946372513903)
XLA Ops:
  0.6 160.9 %backward.1 = (bf16[1,2,128,1024]{3,2,1,0:T(8,128)(2,1)}, bf16[1,2,128,1024]{3,2,1,0:T(8,128)(2,1)}, bf16[1,2,128,1024]{3,2,1,0:T(8,128)(2,1)}) custom-call(bf16[1,2,128,1024]{3,2,1,0:T(8,128)(2,1)} %x.1, bf16[1,2,128,1024]{3,2,1,0:T(8,128)(2,1)} %q.1, bf16[1,2,128,1024]{3,2,1,0:T(8,128)(2,1)} %k.1, bf16[1,16,1024]{2,1,0:T(8,128)(2,1)} %wv.1, ...), custom_call_target="tpu_custom_call" | custom-call | flops 4000000000 | bytes 8388608 | tf_op jit(solution)/shard_map/backward/pallas_call | solution.py:695
  161.5 0.0 copy-start.1
  161.5 1.9 %copy.12 = bf16[1,2,128,1024]{3,2,1,0:T(8,128)(2,1)} copy(bf16[1,2,128,1024]{3,2,1,0:T(8,128)(2,1)} %get-tuple-element.6) | data formatting | bytes 1048576
  163.5 0.0 copy-done.1
  163.5 0.0 copy-start
  163.5 0.8 copy.13
  164.3 0.4 copy-done
  164.7 0.8 copy.14
Async XLA Ops:
  161.5 1.9 %copy-start.1 = (bf16[1,2,128,1024]{3,2,1,0:T(8,128)(2,1)S(1)}, bf16[1,2,128,1024]{3,2,1,0:T(8,128)(2,1)}, u32[]{:S(2)}) copy-start(bf16[1,2,128,1024]{3,2,1,0:T(8,128)(2,1)} %get-tuple-element.7) | copy-start | bytes 1572868
  163.5 1.2 copy-start
